TPU v7x, 32 devices: a whole 2x2x4 slice. The times are simulated.
32 devices in a mesh: dp: 8 (over y, x, core), tm: 4 (over z).
Axes of the slice: x: 2, y: 2, z: 4, core: 2. Of those that a mesh axis runs over, the one named last changes fastest.
Arguments:
- volume: bfloat16 [16, 32, 14, 14, 512], P('dp', 'tm'), may hold values from -6 to 6
- segments: int32 [16, 32], P('dp'), may hold values from 0 to 3, as said below
- keep: int32 [16, 2, 8], P('dp'), may hold values 0 or 1
- ln1_gain: float32 [512], replicated, may hold values from 0.1 to 1.9
- ln1_bias: float32 [512], replicated, may hold values from -1.75 to 1.75
- w_qkv: bfloat16 [512, 1536], replicated, may hold values from -0.25 to 0.25
- q_bias: float32 [512], replicated, may hold values from -3 to 3
- v_bias: float32 [512], replicated, may hold values from -3 to 3
- rel_table: float32 [2535, 16], replicated, may hold values from -6 to 6
- w_proj: bfloat16 [512, 512], replicated, may hold values from -2 to 2
- proj_bias: float32 [512], replicated, may hold values from -1.75 to 1.75
- ln2_gain: float32 [512], replicated, may hold values from 0.1 to 1.9
- ln2_bias: float32 [512], replicated, may hold values from -1.75 to 1.75
- w_fc1: bfloat16 [512, 2048], replicated, may hold values from -0.25 to 0.25
- fc1_bias: float32 [2048], replicated, may hold values from -3 to 3
- w_fc2: bfloat16 [2048, 512], replicated, may hold values from -0.125 to 0.125
- fc2_bias: float32 [512], replicated, may hold values from -1.75 to 1.75
- cotangent: bfloat16 [16, 32, 14, 14, 512], P('dp', 'tm'), may hold values from -6 to 6
Outputs:
- mixed_out: bfloat16 [16, 32, 14, 14, 512], P('dp', 'tm')
- volume_grad: float32 [16, 32, 14, 14, 512], P('dp', 'tm')
- ln1_gain_grad: float32 [512], replicated
- ln1_bias_grad: float32 [512], replicated
- w_qkv_grad: float32 [512, 1536], replicated
- q_bias_grad: float32 [512], replicated
- v_bias_grad: float32 [512], replicated
- rel_table_grad: float32 [2535, 16], replicated
- w_proj_grad: float32 [512, 512], replicated
- proj_bias_grad: float32 [512], replicated
- ln2_gain_grad: float32 [512], replicated
- ln2_bias_grad: float32 [512], replicated
- w_fc1_grad: float32 [512, 2048], replicated
- fc1_bias_grad: float32 [2048], replicated
- w_fc2_grad: float32 [2048, 512], replicated
- fc2_bias_grad: float32 [512], replicated
Inputs may be any that keep to these rules, and one draw needn't show every extreme that they name: `segments`: in every volume the clip numbers start at 0 on the first frame and rise by one at each new clip; every clip but the last has 4 to 8 frames, and the numbering stops at min(7, 3), the last clip taking the remaining frames.
All inputs are finite; a program needn't handle non-finite values. No bound on the sum of `keep` on one device may be relied on, other than what follows from the above.
Results may differ from a plain program's by a relative error of at most 0.011.
Values may be sent and summed in bfloat16 or wider, within the bound.
No kernel may reach another device: no remote copies, remote signals or barrier semaphores. Data moves between devices by JAX's collectives and lax.ppermute only.
A program may use at most 576 MiB of HBM per device.

v0:
```python
import jax
import jax.numpy as jnp
import numpy as np
from jax import lax
from jax.sharding import PartitionSpec as P

SIDE = 14
WT = 8
WIN_HW = 7
SHIFT_T = 4
SHIFT_HW = 3


EPS = 1e-05
KEEP_RATE = 0.75
PRECISE = lax.Precision.HIGHEST


def passed_along(block, axis, distance):
    devices = range(lax.axis_size(axis))
    route = [((i - distance) % len(devices), i) for i in devices]
    return lax.ppermute(block, axis, route)


def layer_norm(values, scaling, offset):
    centre = values - jnp.mean(values, axis=-1, keepdims=True)
    spread = jnp.mean(centre * centre, axis=-1, keepdims=True)
    return centre * lax.rsqrt(spread + EPS) * scaling + offset


def exact_gelu(values):
    return jax.nn.gelu(values, approximate=False)


def offset_hot(span):
    places = jnp.arange(span)
    return (
        places[:, None, None] - places[None, :, None] + span - 1
        == jnp.arange(2 * span - 1)[None, None, :]
    ).astype(jnp.float32)


def region_table(side_len, side_win, shift_hw):
    places = np.arange(side_len)
    region_marks = (places >= side_len - side_win).astype(np.int32) + (
        places >= side_len - shift_hw
    ).astype(np.int32)
    region = region_marks[:, None] * 3 + region_marks[None, :]
    per_side = side_len // side_win
    windows = region.reshape(per_side, side_win, per_side, side_win).transpose(0, 2, 1, 3)
    return windows.reshape(per_side * per_side, side_win * side_win)


def to_windows(field_grid):
    channels = field_grid.shape[-1]
    per_time = field_grid.shape[0] // WT
    per_side = field_grid.shape[1] // WIN_HW
    pieces = field_grid.reshape(per_time, WT, per_side, WIN_HW, per_side, WIN_HW, channels)
    pieces = pieces.transpose(0, 2, 4, 1, 3, 5, 6)
    return pieces.reshape(per_time * per_side * per_side, WT * WIN_HW * WIN_HW, channels)


def from_windows(windows, frames):
    channels = windows.shape[-1]
    per_time = frames // WT
    per_side = SIDE // WIN_HW
    pieces = windows.reshape(per_time, per_side, per_side, WT, WIN_HW, WIN_HW, channels)
    return pieces.transpose(0, 3, 1, 4, 2, 5, 6).reshape(frames, SIDE, SIDE, channels)


def outer_sum(left, right):
    return lax.dot_general(
        left.reshape(-1, left.shape[-1]),
        right.reshape(-1, right.shape[-1]),
        (((0,), (0,)), ((), ())),
        preferred_element_type=jnp.float32,
    )


def back_dot(grad_low, weight):
    return lax.dot_general(
        grad_low,
        weight,
        (((grad_low.ndim - 1,), (1,)), ((), ())),
        preferred_element_type=jnp.float32,
    )


def shards(
    volume,
    segments,
    keep,
    ln1_gain,
    ln1_bias,
    w_qkv,
    q_bias,
    v_bias,
    rel_table,
    w_proj,
    proj_bias,
    ln2_gain,
    ln2_bias,
    w_fc1,
    fc1_bias,
    w_fc2,
    fc2_bias,
    cotangent,
):
    batch_rows = volume.shape[0]
    own_frames = volume.shape[1]
    model_width = volume.shape[-1]
    head_count = rel_table.shape[1]
    head_dim = model_width // head_count
    scale_q = head_dim ** (-0.5)
    total_frames = segments.shape[1]
    first_frame = lax.axis_index("tm") * own_frames
    ext_ids = (first_frame + jnp.arange(own_frames + SHIFT_T)) % total_frames
    frame_pick = (ext_ids[:, None] == jnp.arange(total_frames)[None, :]).astype(jnp.int32)
    seg_ext = jnp.sum(segments[:, None, :] * frame_pick[None], axis=2)
    seg_own = seg_ext[:, :own_frames]
    time_key = (seg_ext + 8 * (ext_ids < SHIFT_T).astype(jnp.int32))[:, SHIFT_T:]

    def window_rows(field_grid):
        rolled = jnp.roll(field_grid, (-SHIFT_HW, -SHIFT_HW), axis=(2, 3))
        return to_windows(rolled.reshape((-1,) + field_grid.shape[2:]))

    def unwindow_rows(windows):
        field_grid = from_windows(windows, batch_rows * own_frames).reshape(
            batch_rows, own_frames, SIDE, SIDE, -1
        )
        return jnp.roll(field_grid, (SHIFT_HW, SHIFT_HW), axis=(2, 3))

    inputs = volume.astype(jnp.float32)
    normed, norm1_back = jax.vjp(layer_norm, inputs, ln1_gain, ln1_bias)
    normed_low = normed.astype(jnp.bfloat16)
    qkv_bias = jnp.concatenate([q_bias, jnp.zeros_like(q_bias), v_bias])
    own_qkv = (jnp.dot(normed_low, w_qkv, preferred_element_type=jnp.float32) + qkv_bias).astype(
        jnp.bfloat16
    )
    incoming = passed_along(own_qkv[:, :SHIFT_T], "tm", -1)
    joined = jnp.concatenate([own_qkv[:, SHIFT_T:], incoming], axis=1)
    windows = window_rows(joined)
    window_count = windows.shape[0]
    wtok = windows.shape[1]
    per_block = max(
        (factor for factor in range(1, -(-512 // wtok) + 1) if window_count % factor == 0)
    )
    blocks = windows.reshape(window_count // per_block, per_block, wtok, 3 * model_width)
    regions = jnp.asarray(region_table(SIDE, WIN_HW, SHIFT_HW))
    combos = (time_key.reshape(-1, 1, WT, 1) * 9 + regions[None, :, None, :]).reshape(
        window_count // per_block, per_block, wtok
    )
    across = 2 * WIN_HW - 1
    hot_t = offset_hot(WT)
    hot_s = offset_hot(WIN_HW)
    cube = rel_table.reshape(2 * WT - 1, across, across, head_count)
    spread_w = jnp.einsum("abch,wvc->abwvh", cube, hot_s, precision=PRECISE)
    spread_h = jnp.einsum("abwvh,ygb->aygwvh", spread_w, hot_s, precision=PRECISE)
    spread_t = jnp.einsum("aygwvh,tsa->tsygwvh", spread_h, hot_t, precision=PRECISE)
    pos_bias = jnp.transpose(spread_t, (6, 0, 2, 4, 1, 3, 5)).reshape(head_count, wtok, wtok)

    def split_heads(packed):
        parts = packed.reshape(packed.shape[0], wtok, 3, head_count, head_dim)
        return (parts[:, :, 0], parts[:, :, 1], parts[:, :, 2])

    def scores_of(query_part, key_part, combo_ids):
        raw_scores = (
            jnp.einsum("gqhd,gkhd->ghqk", query_part, key_part, preferred_element_type=jnp.float32)
            * scale_q
            + pos_bias[None]
        )
        allowed = (combo_ids[:, :, None] == combo_ids[:, None, :])[:, None]
        return jnp.where(allowed, raw_scores, -jnp.inf)

    def forward_block(inputs_pair):
        packed, combo_ids = inputs_pair
        query_part, key_part, value_part = split_heads(packed)
        scores = scores_of(query_part, key_part, combo_ids)
        row_max = jnp.max(scores, axis=-1, keepdims=True)
        exp_scores = jnp.exp(scores - row_max)
        totals = jnp.sum(exp_scores, axis=-1, keepdims=True)
        prob_low = (exp_scores / totals).astype(jnp.bfloat16)
        attended = jnp.einsum(
            "ghqk,gkhd->gqhd", prob_low, value_part, preferred_element_type=jnp.float32
        )
        return (
            attended.astype(jnp.bfloat16).reshape(packed.shape[0], wtok, model_width),
            row_max + jnp.log(totals),
        )

    attended_win, log_totals = lax.map(forward_block, (blocks, combos))
    attended_ext = unwindow_rows(attended_win.reshape(window_count, wtok, model_width))
    back_in = passed_along(attended_ext[:, own_frames - SHIFT_T :], "tm", 1)
    attn_own = jnp.concatenate([back_in, attended_ext[:, : own_frames - SHIFT_T]], axis=1)
    seg_hot = (seg_own[:, :, None] == jnp.arange(8)[None, None, :]).astype(jnp.float32)
    keep_float = keep.astype(jnp.float32)
    drop_attn = (jnp.sum(seg_hot * keep_float[:, 0, :][:, None, :], axis=-1) / KEEP_RATE)[
        :, :, None, None, None
    ]
    drop_mlp = (jnp.sum(seg_hot * keep_float[:, 1, :][:, None, :], axis=-1) / KEEP_RATE)[
        :, :, None, None, None
    ]
    branch = jnp.dot(attn_own, w_proj, preferred_element_type=jnp.float32) + proj_bias
    middle = inputs + drop_attn * branch
    normed2, norm2_back = jax.vjp(layer_norm, middle, ln2_gain, ln2_bias)
    normed2_low = normed2.astype(jnp.bfloat16)
    hidden = jnp.dot(normed2_low, w_fc1, preferred_element_type=jnp.float32) + fc1_bias
    active, gelu_back = jax.vjp(exact_gelu, hidden)
    active_low = active.astype(jnp.bfloat16)
    result = jnp.dot(active_low, w_fc2, preferred_element_type=jnp.float32) + fc2_bias
    mixed_out = (middle + drop_mlp * result).astype(jnp.bfloat16)
    upstream = cotangent.astype(jnp.float32)
    result_grad = (drop_mlp * upstream).astype(jnp.bfloat16)
    fc2_grad = outer_sum(active_low, result_grad)
    fc2_bias_grad = jnp.sum(result_grad, axis=(0, 1, 2, 3), dtype=jnp.float32)
    active_grad = back_dot(result_grad, w_fc2)
    hidden_grad = gelu_back(active_grad)[0].astype(jnp.bfloat16)
    fc1_grad = outer_sum(normed2_low, hidden_grad)
    fc1_bias_grad = jnp.sum(hidden_grad, axis=(0, 1, 2, 3), dtype=jnp.float32)
    normed2_grad = back_dot(hidden_grad, w_fc1)
    middle_grad_ln, ln2_gain_grad, ln2_bias_grad = norm2_back(normed2_grad)
    middle_grad = upstream + middle_grad_ln
    branch_grad = (drop_attn * middle_grad).astype(jnp.bfloat16)
    proj_grad = outer_sum(attn_own, branch_grad)
    proj_bias_grad = jnp.sum(branch_grad, axis=(0, 1, 2, 3), dtype=jnp.float32)
    attn_grad = back_dot(branch_grad, w_proj).astype(jnp.bfloat16)
    ahead = passed_along(attn_grad[:, :SHIFT_T], "tm", -1)
    attn_grad_ext = jnp.concatenate([attn_grad[:, SHIFT_T:], ahead], axis=1)
    grad_win = window_rows(attn_grad_ext).reshape(
        window_count // per_block, per_block, wtok, model_width
    )

    def backward_block(bias_total, inputs_pack):
        packed, combo_ids, log_sums, out_grad = inputs_pack
        query_part, key_part, value_part = split_heads(packed)
        scores = scores_of(query_part, key_part, combo_ids)
        probs_full = jnp.exp(scores - log_sums)
        grad_heads = out_grad.reshape(per_block, wtok, head_count, head_dim)
        value_grad = jnp.einsum(
            "ghqk,gqhd->gkhd",
            probs_full.astype(jnp.bfloat16),
            grad_heads,
            preferred_element_type=jnp.float32,
        )
        prob_grad = jnp.einsum(
            "gqhd,gkhd->ghqk", grad_heads, value_part, preferred_element_type=jnp.float32
        )
        inner_sum = jnp.sum(prob_grad * probs_full, axis=-1, keepdims=True)
        score_grad = (probs_full * (prob_grad - inner_sum)).astype(jnp.bfloat16)
        query_grad = (
            jnp.einsum("ghqk,gkhd->gqhd", score_grad, key_part, preferred_element_type=jnp.float32)
            * scale_q
        )
        key_grad = (
            jnp.einsum(
                "ghqk,gqhd->gkhd", score_grad, query_part, preferred_element_type=jnp.float32
            )
            * scale_q
        )
        stacked = jnp.stack([query_grad, key_grad, value_grad], axis=2).astype(jnp.bfloat16)
        return (
            bias_total + jnp.sum(score_grad, axis=0, dtype=jnp.float32),
            stacked.reshape(per_block, wtok, 3 * model_width),
        )

    bias_total, qkv_grad_win = lax.scan(
        backward_block,
        jnp.zeros((head_count, wtok, wtok), jnp.float32),
        (blocks, combos, log_totals, grad_win),
    )
    bias_grid = bias_total.reshape(head_count, WT, WIN_HW, WIN_HW, WT, WIN_HW, WIN_HW)
    fold_w = jnp.einsum("htywsgv,wvc->htysgc", bias_grid, hot_s, precision=PRECISE)
    fold_h = jnp.einsum("htysgc,ygb->htsbc", fold_w, hot_s, precision=PRECISE)
    fold_t = jnp.einsum("htsbc,tsa->abch", fold_h, hot_t, precision=PRECISE)
    table_grad = fold_t.reshape(-1, head_count)
    qkv_grad_ext = unwindow_rows(qkv_grad_win.reshape(window_count, wtok, 3 * model_width))
    returned = passed_along(qkv_grad_ext[:, own_frames - SHIFT_T :], "tm", 1)
    qkv_grad_own = jnp.concatenate([returned, qkv_grad_ext[:, : own_frames - SHIFT_T]], axis=1)
    normed_grad = back_dot(qkv_grad_own, w_qkv)
    qkv_grad = outer_sum(normed_low, qkv_grad_own)
    column_sums = jnp.sum(qkv_grad_own, axis=(0, 1, 2, 3), dtype=jnp.float32)
    q_bias_grad = column_sums[:model_width]
    v_bias_grad = column_sums[2 * model_width :]
    input_grad_ln, ln1_gain_grad, ln1_bias_grad = norm1_back(normed_grad)
    volume_grad = middle_grad + input_grad_ln
    (
        ln1_gain_total,
        ln1_bias_total,
        qkv_total,
        q_bias_total,
        v_bias_total,
        table_total,
        proj_total,
        proj_bias_total,
        ln2_gain_total,
        ln2_bias_total,
        fc1_total,
        fc1_bias_total,
        fc2_total,
        fc2_bias_total,
    ) = lax.psum(
        (
            ln1_gain_grad,
            ln1_bias_grad,
            qkv_grad,
            q_bias_grad,
            v_bias_grad,
            table_grad,
            proj_grad,
            proj_bias_grad,
            ln2_gain_grad,
            ln2_bias_grad,
            fc1_grad,
            fc1_bias_grad,
            fc2_grad,
            fc2_bias_grad,
        ),
        ("dp", "tm"),
    )
    return (
        mixed_out,
        volume_grad,
        ln1_gain_total,
        ln1_bias_total,
        qkv_total,
        q_bias_total,
        v_bias_total,
        table_total,
        proj_total,
        proj_bias_total,
        ln2_gain_total,
        ln2_bias_total,
        fc1_total,
        fc1_bias_total,
        fc2_total,
        fc2_bias_total,
    )


def solution(mesh):
    return jax.shard_map(
        shards,
        mesh=mesh,
        in_specs=(
            P("dp", "tm", None, None, None),
            P("dp", None),
            P("dp", None, None),
            P(),
            P(),
            P(),
            P(),
            P(),
            P(),
            P(),
            P(),
            P(),
            P(),
            P(),
            P(),
            P(),
            P(),
            P("dp", "tm", None, None, None),
        ),
        out_specs=(
            P("dp", "tm", None, None, None),
            P("dp", "tm", None, None, None),
            P(),
            P(),
            P(),
            P(),
            P(),
            P(),
            P(),
            P(),
            P(),
            P(),
            P(),
            P(),
            P(),
            P(),
        ),
        check_vma=False,
    )
```

profile of v0, /device:TPU:0, one launch (start us, length us, event | category | flops | bytes accessed | tf_op | source)
XLA Modules:
  0.0 2366.3 jit_solution(379302550839596998)
XLA Ops:
  62.6 17.5 convolution_bitcast_fusion.2
  80.1 39.4 %convolution_bitcast_fusion = f32[16,8,7,7,8,7,7]{0,4,6,3,5,2,1:T(8,128)} fusion(f32[15,7,7,7,7,16]{5,2,4,3,0,1:T(8,128)} %convolution_bitcast_fusion.2, pred[8,8,15,1,1,1,1]{2,0,1,6,5,4,3:T(8,128)(4,1)S(1)} %fusion.80), kind=kOutput, calls=%fused_computation.60 | convolution fusion | flops 442552320 | bytes 12140416 | tf_op jit(solution)/shard_map/aygwvh,tsa->tsygwvh/dot_general | solution.py:159
  119.5 56.6 %copy.163 = f32[16,8,7,7,8,7,7]{0,6,5,4,3,2,1:T(8,128)} copy(f32[16,8,7,7,8,7,7]{0,4,6,3,5,2,1:T(8,128)} %convolution_bitcast_fusion) | data formatting | bytes 19668992 | tf_op jit(solution)/shard_map/while | solution.py:191
  176.1 85.5 %add.361 = f32[16,392,392]{0,2,1:T(8,128)} reshape(f32[16,8,7,7,8,7,7]{0,6,5,4,3,2,1:T(8,128)} %copy.163) | data formatting | bytes 19668992 | tf_op jit(solution)/shard_map/while/body/eval_jaxpr/add | solution.py:168
  319.4 30.3 %copy.162 = bf16[4,2,392,1536]{2,3,1,0:T(8,128)(2,1)} copy(bf16[4,2,392,1536]{3,1,2,0:T(2,128)(2,1)} %bitcast.313) | data formatting | bytes 19267584 | tf_op jit(solution)/shard_map/while | solution.py:191
  349.7 408.3 %while.27 = (s32[]{:T(128)}, bf16[4,2,392,512]{3,1,2,0:T(2,128)(2,1)}, f32[4,2,16,392,1]{3,2,1,4,0:T(8,128)}, bf16[4,2,392,1536]{2,3,1,0:T(8,128)(2,1)}, s32[4,2...) while((s32[]{:T(128)}, ...), condition=%wide.wide.region_7.8_spmd, body=%wide.wide.region_4.7_spmd.sunk | while | flops 674359168 | bytes 110560792 | solution.py:191
  353.9 54.4 %copy.285 = f32[16,392,392]{1,2,0:T(8,128)} copy(f32[16,392,392]{0,2,1:T(8,128)} %get-tuple-element.522) | data formatting | bytes 19668992 | tf_op jit(solution)/shard_map/while/body/eval_jaxpr/add | solution.py:168
  455.9 54.4 %copy.285 = f32[16,392,392]{1,2,0:T(8,128)} copy(f32[16,392,392]{0,2,1:T(8,128)} %get-tuple-element.522) | data formatting | bytes 19668992 | tf_op jit(solution)/shard_map/while/body/eval_jaxpr/add | solution.py:168
  558.0 54.4 %copy.285 = f32[16,392,392]{1,2,0:T(8,128)} copy(f32[16,392,392]{0,2,1:T(8,128)} %get-tuple-element.522) | data formatting | bytes 19668992 | tf_op jit(solution)/shard_map/while/body/eval_jaxpr/add | solution.py:168
  660.0 54.4 %copy.285 = f32[16,392,392]{1,2,0:T(8,128)} copy(f32[16,392,392]{0,2,1:T(8,128)} %get-tuple-element.522) | data formatting | bytes 19668992 | tf_op jit(solution)/shard_map/while/body/eval_jaxpr/add | solution.py:168
  767.4 85.9 %add.365 = f32[16,392,392]{0,2,1:T(8,128)} reshape(f32[16,8,7,7,8,7,7]{0,6,5,4,3,2,1:T(8,128)} %copy.163) | data formatting | bytes 19668992 | tf_op jit(solution)/shard_map/while/body/eval_jaxpr/add | solution.py:168
  867.1 23.3 fusion.25
  890.4 69.4 %multiply_convert_fusion.3 = (bf16[2,8,14,14,2048]{4,3,2,1,0:T(8,128)(2,1)}, f32[2,8,14,14,2048]{4,3,2,1,0:T(8,128)}) fusion(f32[2,8,14,14,2048]{4,3,2,1,0:T(8,128)} %get-tuple-element.321, f32[2048]{0:T(1024)S(1)} %copy-done.42, u16[2,8,14,2048]{3,2,1,0:T(8,128)(2,1)S(1)} %get-tuple-element.244, u16[2,8,14,2048]{3,2,1,0:T(8,128)(2,1)S(1)} %get-tuple-element.243), kind=kLoop, calls=%fused_computation.47 | loop fusion | flops 455999488 | bytes 66068480 | tf_op jit(solution)/shard_map/convert_element_type | solution.py:209
  959.8 30.2 %convert_reduce_fusion.1 = (f32[2048]{0:T(1024)}, bf16[2,8,14,14,2048]{4,3,2,1,0:T(8,128)(2,1)}) fusion(f32[2,8,14,14,2048]{4,3,2,1,0:T(8,128)} %get-tuple-element.303, bf16[2048,512]{1,0:T(8,128)(2,1)} %param.38, f32[2,8]{1,0:T(2,128)S(1)} %broadcast_multiply_fusion.2, bf16[2,8,14,14,512]{4,1,3,2,0:T(8,128)(2,1)} %param.40, ...), kind=kOutput, calls=%fused_computation.45 | convolution fusion | flops 6690666496 | bytes 69550144 | tf_op jit(solution)/shard_map/dot_general | solution.py:81
  1072.0 733.8 %while.28 = (s32[]{:T(128)}, f32[16,392,392]{1,2,0:T(8,128)}, bf16[4,2,392,1536]{3,1,2,0:T(2,128)(2,1)}, s32[4,2,392]{2,1,0:T(2,128)}, bf16[4,2,392,1536]{2,3,1,...) while((s32[]{:T(128)}, f32[16,392,392]{1,2,0:T(8,128)}, ...), condition=%wide.wide.region_16.17_spmd.clone, body=%wide.wide.region_13.16_spmd.clone.sunk | while | flops 1639695232 | bytes 272452704 | solution.py:266
  1081.2 54.4 %copy.287 = f32[16,392,392]{1,2,0:T(8,128)} copy(f32[16,392,392]{0,2,1:T(8,128)} %get-tuple-element.554) | data formatting | bytes 19668992 | tf_op jit(solution)/shard_map/while/body/eval_jaxpr/add | solution.py:168
  1154.1 17.3 multiply_reduce_fusion.7
  1171.4 28.7 %convert_reduce_fusion.8 = (f32[16,392,392]{1,2,0:T(8,128)}, bf16[2,16,392,392]{2,3,1,0:T(8,128)(2,1)}) fusion(f32[2,16,392,392]{2,3,1,0:T(8,128)} %subtract_exponential_fusion.4, f32[2,16,392,392]{2,3,1,0:T(8,128)} %get-tuple-element.496, f32[2,16,392]{2,1,0:T(8,128)S(1)} %get-tuple-element.497), kind=kLoop, calls=%fused_computation.14.clone.clone.1 | loop fusion | flops 22127616 | bytes 59057152 | tf_op jit(solution)/shard_map/while/body/eval_jaxpr/reduce_sum | solution.py:262
  1261.7 54.4 %copy.287 = f32[16,392,392]{1,2,0:T(8,128)} copy(f32[16,392,392]{0,2,1:T(8,128)} %get-tuple-element.554) | data formatting | bytes 19668992 | tf_op jit(solution)/shard_map/while/body/eval_jaxpr/add | solution.py:168
  1351.9 28.7 %convert_reduce_fusion.8 = (f32[16,392,392]{1,2,0:T(8,128)}, bf16[2,16,392,392]{2,3,1,0:T(8,128)(2,1)}) fusion(f32[2,16,392,392]{2,3,1,0:T(8,128)} %subtract_exponential_fusion.4, f32[2,16,392,392]{2,3,1,0:T(8,128)} %get-tuple-element.496, f32[2,16,392]{2,1,0:T(8,128)S(1)} %get-tuple-element.497), kind=kLoop, calls=%fused_computation.14.clone.clone.1 | loop fusion | flops 22127616 | bytes 59057152 | tf_op jit(solution)/shard_map/while/body/eval_jaxpr/reduce_sum | solution.py:262
  1444.9 54.4 %copy.287 = f32[16,392,392]{1,2,0:T(8,128)} copy(f32[16,392,392]{0,2,1:T(8,128)} %get-tuple-element.554) | data formatting | bytes 19668992 | tf_op jit(solution)/shard_map/while/body/eval_jaxpr/add | solution.py:168
  1535.1 28.7 %convert_reduce_fusion.8 = (f32[16,392,392]{1,2,0:T(8,128)}, bf16[2,16,392,392]{2,3,1,0:T(8,128)(2,1)}) fusion(f32[2,16,392,392]{2,3,1,0:T(8,128)} %subtract_exponential_fusion.4, f32[2,16,392,392]{2,3,1,0:T(8,128)} %get-tuple-element.496, f32[2,16,392]{2,1,0:T(8,128)S(1)} %get-tuple-element.497), kind=kLoop, calls=%fused_computation.14.clone.clone.1 | loop fusion | flops 22127616 | bytes 59057152 | tf_op jit(solution)/shard_map/while/body/eval_jaxpr/reduce_sum | solution.py:262
  1628.1 54.4 %copy.287 = f32[16,392,392]{1,2,0:T(8,128)} copy(f32[16,392,392]{0,2,1:T(8,128)} %get-tuple-element.554) | data formatting | bytes 19668992 | tf_op jit(solution)/shard_map/while/body/eval_jaxpr/add | solution.py:168
  1701.0 17.3 multiply_reduce_fusion.7
  1718.3 28.7 %convert_reduce_fusion.8 = (f32[16,392,392]{1,2,0:T(8,128)}, bf16[2,16,392,392]{2,3,1,0:T(8,128)(2,1)}) fusion(f32[2,16,392,392]{2,3,1,0:T(8,128)} %subtract_exponential_fusion.4, f32[2,16,392,392]{2,3,1,0:T(8,128)} %get-tuple-element.496, f32[2,16,392]{2,1,0:T(8,128)S(1)} %get-tuple-element.497), kind=kLoop, calls=%fused_computation.14.clone.clone.1 | loop fusion | flops 22127616 | bytes 59057152 | tf_op jit(solution)/shard_map/while/body/eval_jaxpr/reduce_sum | solution.py:262
  1823.5 46.1 %copy.184 = f32[16,392,392]{0,2,1:T(8,128)} copy(f32[16,392,392]{1,2,0:T(8,128)} %get-tuple-element.95) | data formatting | bytes 19668992 | tf_op jit(solution)/shard_map/while | solution.py:266
  1869.6 86.0 %reshape.284 = f32[16,8,7,7,8,7,7]{0,6,5,4,3,2,1:T(8,128)} reshape(f32[16,392,392]{0,2,1:T(8,128)} %copy.184) | data formatting | bytes 19668992 | tf_op jit(solution)/shard_map/reshape | solution.py:271
  1984.2 49.4 %convolution_bitcast_fusion.1 = f32[16,8,7,8,7,13]{0,5,4,3,2,1:T(8,128)} fusion(f32[16,8,7,7,8,7,7]{0,6,5,4,3,2,1:T(8,128)} %reshape.284, s32[7,7]{1,0:T(8,128)S(1)} %copy-done.36), kind=kOutput, calls=%fused_computation.89 | convolution fusion | flops 383545984 | bytes 12443844 | tf_op jit(solution)/shard_map/htywsgv,wvc->htysgc/dot_general | solution.py:272
  2033.6 29.7 %fusion.51 = f32[16,8,8,13,13]{0,3,4,2,1:T(8,128)S(1)} fusion(f32[16,8,7,8,7,13]{0,5,4,3,2,1:T(8,128)} %convolution_bitcast_fusion.1, s32[7,7]{1,0:T(8,128)S(1)} %copy-done.36), kind=kOutput, calls=%fused_computation.133 | convolution fusion | flops 101757568 | bytes 3301572 | tf_op jit(solution)/shard_map/htysgc,ygb->htsbc/dot_general | solution.py:273
  2071.8 19.3 collective-permute-done.3
  2180.8 39.5 %all-reduce = (f32[512]{0:T(512)}, f32[512]{0:T(512)}, f32[512]{0:T(512)}, f32[512]{0:T(512)}, f32[512]{0:T(512)}, /*index=5*/f32[512]{0:T(512)}, f32[512]{0:T(512)}, f32[2048]{0:T(1024)}, f32[512]{0:T(512)}) all-reduce(f32[512]{0:T(512)S(1)} %get-tuple-element.247, ...), channel_id=1, replica_groups=mesh['dp'=8,'tm'=4] {'dp','tm'}, use_global_device_ids=true, to_apply=%region_20.21 | all-reduce | flops 6144 | bytes 49152 | tf_op jit(solution)/shard_map/psum | solution.py:301
  2220.4 127.5 %all-reduce.4.cloned.1.call-done = (f32[512,1536]{1,0:T(8,128)}, f32[2535,16]{0,1:T(8,128)}, f32[512,512]{1,0:T(8,128)}, f32[512,2048]{1,0:T(8,128)}, f32[2048,512]{1,0:T(8,128)}) async-done(((f32[512,1536]{1,0:T(8,128)}, f32[2535,16]{0,1:T(8,128)}, f32[512,512]{1,0:T(8,128)}, f32[512,2048]{1,0:T(8,128)}, f32[2048,512]{1,0:T(8,128)}), (f32[512,1536]{1,0:T(8,128)}, f32[2535,16]{0,1:T(8,128)}, ...) | async-done | bytes 12745168 | tf_op jit(solution)/shard_map/psum | solution.py:301
  (366 shorter events, 926.3 us)
Async XLA Ops:
  7.2 859.8 %copy-start = (bf16[512,2048]{1,0:T(8,128)(2,1)S(1)}, bf16[512,2048]{1,0:T(8,128)(2,1)}, u32[]{:S(2)}) copy-start(bf16[512,2048]{1,0:T(8,128)(2,1)} %param.36) | copy-start | bytes 6291460
  7.2 2340.7 %all-reduce.4.cloned.1.call-start = ((), (), s32[]{:S(2)}) async-start(), calls=%async_computation | async-start | bytes 25493504 | tf_op jit(solution)/shard_map/psum | solution.py:301
  47.0 216.1 %collective-permute-start = (bf16[2,4,14,14,1536]{4,1,3,2,0:T(4,128)(2,1)}, bf16[2,4,14,14,1536]{4,1,3,2,0:T(4,128)(2,1)}, u32[]{:S(2)}, u32[]{:S(2)}) collective-permute-start(bf16[2,4,14,14,1536]{4,1,3,2,0:T(4,128)(2,1)} %copy.153), channel_id=1, source_target_pairs={{1,0},{2,1},{3,2},{0,3},{5,4},{6,5},{7,6},{4,7},{9,8},{10,9},{11,1... | collective-permute-start | bytes 14450696 | tf_op jit(solution)/shard_map/ppermute | solution.py:22
  52.0 28.0 %copy-start.35 = (s32[7,7]{1,0:T(8,128)}, s32[7,7]{1,0:T(8,128)S(1)}, u32[]{:S(2)}) copy-start(s32[7,7]{1,0:T(8,128)S(1)} %subtract_add_fusion) | copy-start | bytes 592
  52.0 28.0 %copy-start.39 = (s32[8,8]{0,1:T(8,128)}, s32[8,8]{0,1:T(8,128)S(1)}, u32[]{:S(2)}) copy-start(s32[8,8]{0,1:T(8,128)S(1)} %subtract_add_fusion.1) | copy-start | bytes 772
  176.1 85.7 %copy-start.58 = (s32[2,32]{1,0:T(2,128)S(1)}, s32[2,32]{1,0:T(2,128)}, u32[]{:S(2)}) copy-start(s32[2,32]{1,0:T(2,128)} %param.24) | copy-start | bytes 772
  176.1 86.8 %copy-start.56 = (s32[4,49]{1,0:T(4,128)S(1)}, s32[4,49]{1,0:T(4,128)}, u32[]{:S(2)}) copy-start(s32[4,49]{1,0:T(4,128)} %constant.170.clone) | copy-start | bytes 2356
  762.4 93.1 %copy-start.18 = (bf16[2,8,14,3,512]{4,3,2,1,0:T(4,128)(2,1)}, bf16[2,8,14,3,512]{4,3,2,1,0:T(4,128)(2,1)S(1)}, u32[]{:S(2)}) copy-start(bf16[2,8,14,3,512]{4,3,2,1,0:T(4,128)(2,1)S(1)} %slice.174) | copy-start | bytes 2064388
  767.3 86.0 %copy-start.41 = (s32[2,8]{0,1:T(8,128)S(1)}, s32[2,8]{0,1:T(8,128)}, u32[]{:S(2)}) copy-start(s32[2,8]{0,1:T(8,128)} %get-tuple-element.316) | copy-start | bytes 196
  767.3 86.1 %copy-start.57 = (s32[2,2,8]{2,1,0:T(2,128)S(1)}, s32[2,2,8]{2,1,0:T(2,128)}, u32[]{:S(2)}) copy-start(s32[2,2,8]{2,1,0:T(2,128)} %param.25) | copy-start | bytes 388
  767.3 88.2 %copy-start.60 = (bf16[512,512]{1,0:T(8,128)(2,1)S(1)}, bf16[512,512]{1,0:T(8,128)(2,1)}, u32[]{:S(2)}) copy-start(bf16[512,512]{1,0:T(8,128)(2,1)} %param.32) | copy-start | bytes 1572868
  767.3 88.2 %copy-start.61 = (f32[512]{0:T(512)S(1)}, f32[512]{0:T(512)}, u32[]{:S(2)}) copy-start(f32[512]{0:T(512)} %param.33) | copy-start | bytes 6148
  767.3 86.3 %collective-permute-start.1 = (bf16[2,4,14,14,512]{4,1,3,2,0:T(4,128)(2,1)}, bf16[2,4,14,14,512]{4,1,3,2,0:T(4,128)(2,1)}, u32[]{:S(2)}, u32[]{:S(2)}) collective-permute-start(bf16[2,4,14,14,512]{4,1,3,2,0:T(4,128)(2,1)} %copy.168), channel_id=1, source_target_pairs={{3,0},{0,1},{1,2},{2,3},{7,4},{4,5},{5,6},{6,7},{11,8},{8,9},{9,10... | collective-permute-start | bytes 4816904 | tf_op jit(solution)/shard_map/ppermute | solution.py:22
  853.6 171.2 %copy-start.48 = (f32[2,8]{1,0:T(2,128)}, f32[2,8]{1,0:T(2,128)S(1)}, u32[]{:S(2)}) copy-start(f32[2,8]{1,0:T(2,128)S(1)} %broadcast_multiply_fusion.2) | copy-start | bytes 196
  862.7 142.7 %copy-start.28 = (f32[2,8,14,14]{3,2,1,0:T(8,128)}, f32[2,8,14,14]{3,2,1,0:T(8,128)S(1)}, u32[]{:S(2)}) copy-start(f32[2,8,14,14]{3,2,1,0:T(8,128)S(1)} %broadcast_multiply_fusion) | copy-start | bytes 37636
  867.0 138.4 %copy-start.33 = (f32[2,8,14,14]{3,2,1,0:T(8,128)}, f32[2,8,14,14]{3,2,1,0:T(8,128)S(1)}, u32[]{:S(2)}) copy-start(f32[2,8,14,14]{3,2,1,0:T(8,128)S(1)} %fusion.78) | copy-start | bytes 37636
  1016.6 26.7 %slice-start.5 = ((s8[7340032]{0:T(1024)(128)(4,1)}), s8[4194304]{0:T(1024)(128)(4,1)S(1)}, s32[]{:S(2)}) async-start(s8[7340032]{0:T(1024)(128)(4,1)} %bitcast.314), calls=%async_computation.6 | async-start | bytes 8388608
  1021.0 38.2 %collective-permute-start.2 = (bf16[2,4,14,14,512]{4,1,3,2,0:T(4,128)(2,1)}, bf16[2,4,14,14,512]{4,1,3,2,0:T(4,128)(2,1)}, u32[]{:S(2)}, u32[]{:S(2)}) collective-permute-start(bf16[2,4,14,14,512]{4,1,3,2,0:T(4,128)(2,1)} %copy.171), channel_id=1, source_target_pairs={{1,0},{2,1},{3,2},{0,3},{5,4},{6,5},{7,6},{4,7},{9,8},{10,9},{11,1... | collective-permute-start | bytes 4816904 | tf_op jit(solution)/shard_map/ppermute | solution.py:22
  1024.8 18.5 slice-start.6
  1171.4 28.7 %copy-start.2 = (bf16[1,2,392,1536]{2,3,1,0:T(8,128)(2,1)S(1)}, bf16[1,2,392,1536]{2,3,1,0:T(8,128)(2,1)}, u32[]{:S(2)}) copy-start(bf16[1,2,392,1536]{2,3,1,0:T(8,128)(2,1)} %constant_dynamic-slice_fusion.10) | copy-start | bytes 7225348 | tf_op jit(solution)/shard_map/while
  1351.9 28.7 %copy-start.2 = (bf16[1,2,392,1536]{2,3,1,0:T(8,128)(2,1)S(1)}, bf16[1,2,392,1536]{2,3,1,0:T(8,128)(2,1)}, u32[]{:S(2)}) copy-start(bf16[1,2,392,1536]{2,3,1,0:T(8,128)(2,1)} %constant_dynamic-slice_fusion.10) | copy-start | bytes 7225348 | tf_op jit(solution)/shard_map/while
  1535.1 28.7 %copy-start.2 = (bf16[1,2,392,1536]{2,3,1,0:T(8,128)(2,1)S(1)}, bf16[1,2,392,1536]{2,3,1,0:T(8,128)(2,1)}, u32[]{:S(2)}) copy-start(bf16[1,2,392,1536]{2,3,1,0:T(8,128)(2,1)} %constant_dynamic-slice_fusion.10) | copy-start | bytes 7225348 | tf_op jit(solution)/shard_map/while
  1718.3 28.7 %copy-start.2 = (bf16[1,2,392,1536]{2,3,1,0:T(8,128)(2,1)S(1)}, bf16[1,2,392,1536]{2,3,1,0:T(8,128)(2,1)}, u32[]{:S(2)}) copy-start(bf16[1,2,392,1536]{2,3,1,0:T(8,128)(2,1)} %constant_dynamic-slice_fusion.10) | copy-start | bytes 7225348 | tf_op jit(solution)/shard_map/while
  1984.1 106.9 %collective-permute-start.3 = (bf16[2,4,14,14,1536]{4,1,3,2,0:T(4,128)(2,1)}, bf16[2,4,14,14,1536]{4,1,3,2,0:T(4,128)(2,1)}, u32[]{:S(2)}, u32[]{:S(2)}) collective-permute-start(bf16[2,4,14,14,1536]{4,1,3,2,0:T(4,128)(2,1)} %copy.182), channel_id=1, source_target_pairs={{3,0},{0,1},{1,2},{2,3},{7,4},{4,5},{5,6},{6,7},{11,8},{8,9},{9,10... | collective-permute-start | bytes 14450696 | tf_op jit(solution)/shard_map/ppermute | solution.py:22
  2033.6 29.8 %copy-start.40 = (s32[8,8]{0,1:T(8,128)S(1)}, s32[8,8]{0,1:T(8,128)}, u32[]{:S(2)}) copy-start(s32[8,8]{0,1:T(8,128)} %copy-done.39) | copy-start | bytes 772
  2068.2 28.9 %copy-start.21 = (f32[2,8,14,14]{3,2,1,0:T(8,128)S(1)}, f32[2,8,14,14]{3,2,1,0:T(8,128)}, u32[]{:S(2)}) copy-start(f32[2,8,14,14]{3,2,1,0:T(8,128)} %copy-done.20) | copy-start | bytes 37636
  2068.2 28.9 %copy-start.44 = (f32[512]{0:T(512)S(1)}, f32[512]{0:T(512)}, u32[]{:S(2)}) copy-start(f32[512]{0:T(512)} %param.26) | copy-start | bytes 6148
  2068.3 28.9 %copy-start.65 = (f32[512]{0:T(512)S(1)}, f32[512]{0:T(512)}, u32[]{:S(2)}) copy-start(f32[512]{0:T(512)} %param.27) | copy-start | bytes 6148
  2070.5 26.6 %copy-start.25 = (f32[2,8,14,14]{3,2,1,0:T(8,128)S(1)}, f32[2,8,14,14]{3,2,1,0:T(8,128)}, u32[]{:S(2)}) copy-start(f32[2,8,14,14]{3,2,1,0:T(8,128)} %copy-done.24) | copy-start | bytes 37636
  2142.8 31.2 %slice-start.2 = ((s8[11010048]{0:T(1024)(128)(4,1)}), s8[4194304]{0:T(1024)(128)(4,1)S(1)}, s32[]{:S(2)}) async-start(s8[11010048]{0:T(1024)(128)(4,1)} %bitcast.307), calls=%async_computation.3 | async-start | bytes 8388608
  2150.8 23.1 slice-start.3
  2150.8 23.1 slice-start.4
  (50 other events, 363.4 us)
Sparse Core Ops, SparseCore 0:
  2110.0 237.8 all-reduce.3
where the time goes:
time: 2390 us; the launch traced here: 2370 us
  local copies, waits for them, and re-layouts  1130 us (47%)
  matrix products  661 us (28%)
  other arithmetic  364 us (15%)
  waiting for transfers between devices  147 us (6%)
  blocking collectives  39.5 us (2%)
    add x10, local copies, waits for them, and re-layouts, scores_of(): jnp.einsum('gqhd,gkhd->ghqk', query_part, key_part, preferred_element_typ...  607 us
    psum x1, waiting for transfers between devices, shards(): lax.psum((ln1_gain_grad, ln1_bias_grad, qkv_grad, q_bias_grad, v_bias_gra...  128 us
    dot_general x8, matrix products, scores_of(): jnp.einsum('gqhd,gkhd->ghqk', query_part, key_part, preferred_element_typ...  122 us
    reduce_sum x4, other arithmetic, backward_block(): jnp.sum(score_grad, axis=0, dtype=jnp.float32)  115 us
    while x2, local copies, waits for them, and re-layouts, shards(): attended_win, log_totals = lax.map(forward_block, (blocks, combos))  86.8 us
    reshape x1, local copies, waits for them, and re-layouts, shards(): bias_total.reshape(head_count, WT, WIN_HW, WIN_HW, WT, WIN_HW, WIN_HW)  86 us
    convert_element_type x1, other arithmetic, shards(): active_low = active.astype(jnp.bfloat16)  69.4 us
    dot_general x4, matrix products, backward_block(): jnp.einsum('gqhd,gkhd->ghqk', grad_heads, value_part, preferred_element_t...  69.3 us
  transfers between devices with their start and end apart: 5, of which 2 were waited for; matrix products, arithmetic and copies ran while one was open for 21% of the time, Pallas kernels for 0%

commit v1 on v0

v1 whole, which is shorter than its diff:
```python
import functools

import jax
import jax.numpy as jnp
import numpy as np
from jax import lax
from jax.experimental import pallas as pl
from jax.experimental.pallas import tpu as pltpu
from jax.sharding import PartitionSpec as P

SIDE = 14
WT = 8
WIN_HW = 7
SHIFT_T = 4
SHIFT_HW = 3
EPS = 1e-05
KEEP_RATE = 0.75
PRECISE = lax.Precision.HIGHEST
LOG2E = 1.4426950408889634
LN2 = 0.6931471805599453
FAR = 1e30
F32 = jnp.float32
BF16 = jnp.bfloat16

SPANS = (
    (SHIFT_HW, WIN_HW),
    (SHIFT_HW + WIN_HW, SIDE - SHIFT_HW - WIN_HW),
    (0, SHIFT_HW),
)
ACROSS = 2 * WIN_HW - 1
RECTS = (
    (0, 0, True, 0),
    (1, 0, True, 0),
    (0, 1, False, 1),
    (2, 0, True, 0),
    (0, 2, False, 1),
    (2, 2, True, 3),
    (2, 1, True, 2),
    (1, 2, True, 3),
    (1, 1, True, 2),
)
BIAS_DIMS = ((7, 7), (4, 7), (4, 4), (4, 3))


def up_to(value, unit):
    return -(-value // unit) * unit


class Rect:
    pass


def plan_rects():
    rects, slots, start = [], [], 0
    class_rows = [0, 0, 0]
    for row_span, col_span, rows_outer, table in RECTS:
        r0, rn = SPANS[row_span]
        c0, cn = SPANS[col_span]
        rect = Rect()
        if rows_outer:
            places = [(r0 + a, c0 + b) for a in range(rn) for b in range(cn)]
        else:
            places = [(r0 + b, c0 + a) for a in range(cn) for b in range(rn)]
        rect.count = len(places) * WT
        rect.rows = up_to(rect.count, 16)
        rect.lanes = up_to(rect.count, 128)
        rect.start = start
        rect.table = table
        rect.kind = {512: 0, 256: 1, 128: 2}[rect.lanes]
        rect.kind_row = class_rows[rect.kind]
        class_rows[rect.kind] += rect.rows
        slots += places + [None] * ((rect.rows - rect.count) // WT)
        start += rect.rows
        rects.append(rect)
    return rects, slots, class_rows


RECT, SLOTS, KIND_ROWS = plan_rects()
TOKENS = len(SLOTS) * WT
KIND_LANES = (512, 256, 128)
ROW_PAD = 16
FRAME_ROWS = SIDE * ROW_PAD


def nn(a, b):
    return lax.dot_general(a, b, (((1,), (0,)), ((), ())), preferred_element_type=F32)


def nt(a, b):
    return lax.dot_general(a, b, (((1,), (1,)), ((), ())), preferred_element_type=F32)


def wide(pattern, width):
    return jnp.concatenate([pattern] * (width // pattern.shape[-1]), axis=-1)


def by_frame(values, pattern):
    rows, width = values.shape
    scaled = values.reshape(rows // WT, WT, width) * wide(pattern, width)[None]
    return scaled.reshape(rows, width)


def column_sums(values):
    rows, width = values.shape
    return jnp.sum(values.reshape(rows // 8, 8, width), axis=0)


def gather_tokens(block_ref, offset, grid32):
    def frame(f, carry):
        base = pl.multiple_of((offset + f) * FRAME_ROWS, ROW_PAD)
        for h in range(SIDE):
            row = block_ref[f, h].astype(F32)
            for part in range(4):
                grid32[part, pl.ds(base + h * ROW_PAD, SIDE), :] = row[:, part * 128 : part * 128 + 128]
        return carry

    lax.fori_loop(0, SHIFT_T, frame, 0)


def grid_to_tokens(grid32, tokens):
    for slot, place in enumerate(SLOTS):
        rows = slice(slot * WT, slot * WT + WT)
        for part in range(4):
            lanes = slice(part * 128, part * 128 + 128)
            if place is None:
                tokens[rows, lanes] = jnp.zeros((WT, 128), F32)
            else:
                at = place[0] * ROW_PAD + place[1]
                tokens[rows, lanes] = grid32[part, pl.ds(at, WT, stride=FRAME_ROWS), :]


def tokens_to_grid(tokens, grid32):
    for slot, place in enumerate(SLOTS):
        if place is None:
            continue
        rows = slice(slot * WT, slot * WT + WT)
        at = place[0] * ROW_PAD + place[1]
        for part in range(4):
            grid32[part, pl.ds(at, WT, stride=FRAME_ROWS), :] = tokens[rows, part * 128 : part * 128 + 128]


def grid_to_frames(grid32, offset, block_ref):
    def frame(f, carry):
        base = pl.multiple_of((offset + f) * FRAME_ROWS, ROW_PAD)
        for h in range(SIDE):
            row = [grid32[part, pl.ds(base + h * ROW_PAD, SIDE), :] for part in range(4)]
            block_ref[f, h] = jnp.concatenate(row, axis=-1).astype(block_ref.dtype)
        return carry

    lax.fori_loop(0, SHIFT_T, frame, 0)


def spread_table(source, outer, inner, out_ref, lane):
    width = inner * WT
    total = outer * width
    for ok in range(outer):
        for ik in range(inner):
            pieces = []
            for oq in range(outer):
                shift = (oq * width - (WIN_HW - 1 - ik) * WT) % 128
                piece = source[oq - ok + WIN_HW - 1]
                pieces.append(pltpu.roll(piece, shift, 1) if shift else piece)
            row = (ok * inner + ik) * WT
            for tile in range(up_to(total, 128) // 128):
                value = None
                for oq in range(outer):
                    begin, end = oq * width, (oq + 1) * width
                    if end <= tile * 128 or begin >= tile * 128 + 128:
                        continue
                    if value is None:
                        value = pieces[oq]
                    else:
                        value = jnp.where(lane >= begin - tile * 128, pieces[oq], value)
                out_ref[0, row : row + WT, tile * 128 : tile * 128 + 128] = value


def bias_kernel(rows_ref, cols_ref, b0_ref, b1_ref, b2_ref, b3_ref):
    lane = lax.broadcasted_iota(jnp.int32, (WT, 128), 1)
    by_rows = [rows_ref[0, d] for d in range(ACROSS)]
    by_cols = [cols_ref[0, d] for d in range(ACROSS)]
    for out_ref, source, (outer, inner) in zip(
        (b0_ref, b1_ref, b2_ref, b3_ref), (by_rows, by_cols, by_rows, by_rows), BIAS_DIMS
    ):
        spread_table(source, outer, inner, out_ref, lane)


def bias_shapes(heads):
    shapes = []
    for outer, inner in BIAS_DIMS:
        count = outer * inner * WT
        shapes.append((heads, count, up_to(count, 128)))
    return shapes


def time_hot():
    places = np.arange(WT)
    hot = places[None, :, None] - places[:, None, None] + WT - 1 == np.arange(2 * WT - 1)[None, None, :]
    return jnp.asarray(hot.astype(np.float32))


def make_bias(rel_table):
    heads = rel_table.shape[1]
    cube = rel_table.reshape(2 * WT - 1, ACROSS, ACROSS, heads) * LOG2E
    both = jnp.einsum("ksd,dabn->nakbs", time_hot(), cube, precision=PRECISE)
    swapped = jnp.einsum("ksd,dabn->nbkas", time_hot(), cube, precision=PRECISE)
    pad = ((0, 0), (0, 0), (0, 0), (0, 128 - ACROSS * WT))
    by_rows = jnp.pad(both.reshape(heads, ACROSS, WT, ACROSS * WT), pad)
    by_cols = jnp.pad(swapped.reshape(heads, ACROSS, WT, ACROSS * WT), pad)
    strip = pl.BlockSpec((1, ACROSS, WT, 128), lambda h: (h, 0, 0, 0))
    shapes = bias_shapes(heads)
    return pl.pallas_call(
        bias_kernel,
        grid=(heads,),
        in_specs=[strip, strip],
        out_specs=[pl.BlockSpec((1,) + s[1:], lambda h: (h, 0, 0)) for s in shapes],
        out_shape=[jax.ShapeDtypeStruct(s, F32) for s in shapes],
        compiler_params=pltpu.CompilerParams(vmem_limit_bytes=48 << 20),
        name="position_bias",
    )(by_rows, by_cols)


def fold_table(acc, outer, inner, totals, lane):
    width = inner * WT
    for ok in range(outer):
        for ik in range(inner):
            row = (ok * inner + ik) * WT
            for oq in range(outer):
                shift = (oq * width - (WIN_HW - 1 - ik) * WT) % 128
                begin, end = oq * width, (oq + 1) * width
                tile, lo = begin // 128, begin % 128
                last = (end - 1) // 128
                value = acc(row, tile)
                if last == tile:
                    value = jnp.where((lane >= lo) & (lane < lo + width), value, 0.0)
                else:
                    after = jnp.where(lane < end - last * 128, acc(row, last), 0.0)
                    value = jnp.where(lane >= lo, value, after)
                d = oq - ok + WIN_HW - 1
                back = pltpu.roll(value, (128 - shift) % 128, 1) if shift else value
                totals[d] = totals[d] + back


def qkv_kernel(
    tile, scale, own_ref, recv_ref, gain_ref, bias_ref, w_ref, wb_ref, x_ref, n_ref, q_ref, k_ref, v_ref, grid32, tokens
):
    win, step = pl.program_id(0), pl.program_id(1)

    @pl.when(step == 0)
    def _():
        gather_tokens(own_ref.at[0], win * SHIFT_T, grid32)
        gather_tokens(recv_ref.at[0], SHIFT_T - win * SHIFT_T, grid32)
        grid_to_tokens(grid32, tokens)

    x = tokens[pl.ds(pl.multiple_of(step * tile, 16), tile), :]
    x_ref[0] = x.astype(BF16)
    centre = x - jnp.mean(x, axis=-1, keepdims=True)
    spread = jnp.mean(centre * centre, axis=-1, keepdims=True)
    normed = (centre * lax.rsqrt(spread + EPS) * gain_ref[...] + bias_ref[...]).astype(BF16)
    n_ref[0] = normed
    width = x.shape[1]
    q_ref[0] = ((nn(normed, w_ref[:, :width]) + wb_ref[:, :width]) * scale).astype(BF16)
    k_ref[0] = nn(normed, w_ref[:, width : 2 * width]).astype(BF16)
    v_ref[0] = (nn(normed, w_ref[:, 2 * width :]) + wb_ref[:, 2 * width :]).astype(BF16)


def whole(shape):
    return pl.BlockSpec(shape, lambda *_: (0,) * len(shape))


def half_spec(side, width):
    return pl.BlockSpec((1, SHIFT_T, side, side, width), lambda w, j: (w, 1 - w, 0, 0, 0))


def other_spec(side, width):
    return pl.BlockSpec((1, SHIFT_T, side, side, width), lambda w, j: (w, 0, 0, 0, 0))


def tile_spec(tile, width):
    return pl.BlockSpec((1, tile, width), lambda w, j: (w, j, 0))


def make_qkv(volume, recv, gain, bias, w_qkv, qkv_bias, scale, tile=400):
    width = volume.shape[-1]
    out = jax.ShapeDtypeStruct((2, TOKENS, width), BF16)
    return pl.pallas_call(
        functools.partial(qkv_kernel, tile, scale),
        grid=(2, TOKENS // tile),
        in_specs=[
            half_spec(SIDE, width),
            other_spec(SIDE, width),
            whole((1, width)),
            whole((1, width)),
            whole(w_qkv.shape),
            whole((1, 3 * width)),
        ],
        out_specs=[tile_spec(tile, width)] * 5,
        out_shape=[out] * 5,
        scratch_shapes=[
            pltpu.VMEM((4, WT * FRAME_ROWS, 128), F32),
            pltpu.VMEM((TOKENS, width), F32),
        ],
        compiler_params=pltpu.CompilerParams(vmem_limit_bytes=60 << 20),
        name="norm1_qkv",
    )(volume, recv, gain[None], bias[None], w_qkv, qkv_bias[None])


def head_rows(transposed, head, dim):
    rows, lanes = transposed.shape
    parts = []
    if head:
        parts.append(jnp.zeros((head * dim, lanes), transposed.dtype))
    parts.append(transposed[head * dim : head * dim + dim])
    if (head + 1) * dim < rows:
        parts.append(jnp.zeros((rows - (head + 1) * dim, lanes), transposed.dtype))
    return jnp.concatenate(parts, axis=0)


def attend_kernel(
    dim, q_ref, k_ref, v_ref, far_ref, b0, b1, b2, b3, e0_ref, e1_ref, e2_ref, o_ref, r_ref, scores
):
    biases = (b0, b1, b2, b3)
    e_refs = (e0_ref, e1_ref, e2_ref)
    far = far_ref[0]
    per = 128 // dim
    for rect in RECT:
        count, rows, lanes, start = rect.count, rect.rows, rect.lanes, rect.start
        kind_rows = slice(rect.kind_row, rect.kind_row + rows)
        e_ref = e_refs[rect.kind]
        queries = q_ref[0, start : start + lanes, :].T
        keys = k_ref[0, start : start + rows, :]
        values = v_ref[0, start : start + rows, :].T
        ones = jnp.ones((16, rows), BF16)
        wide_far = wide(far, lanes)
        outs, scales = [], []
        for head in range(per):
            raw = nn(keys, head_rows(queries, head, dim))[:count]
            raw = raw + biases[rect.table][head, :count, :lanes]
            scores[:count, :lanes] = raw
            blocks = raw.reshape(count // 8, 8, lanes)
            top = jnp.max(blocks, axis=0) - wide_far
            top = jnp.max(top, axis=0, keepdims=True) + wide_far
            exps = jnp.exp2(scores[:count, :lanes].reshape(count // 8, 8, lanes) - top[None])
            exps = exps.reshape(count, lanes).astype(BF16)
            if rows > count:
                exps = jnp.concatenate([exps, jnp.zeros((rows - count, lanes), BF16)], axis=0)
            e_ref[0, 0, kind_rows, head * lanes : head * lanes + lanes] = exps
            lhs = jnp.concatenate([values[head * dim : head * dim + dim], ones], axis=0)
            out = nn(lhs, exps)
            inverse = jnp.broadcast_to(1.0 / out[dim : dim + 1], (dim, lanes))
            outs.append(out[:dim] * inverse)
            scales.append(inverse)
        o_ref[0, start : start + rows, :] = jnp.concatenate(outs, axis=0).T[:rows].astype(BF16)
        r_ref[0, start : start + rows, :] = jnp.concatenate(scales, axis=0).T[:rows]


def head_group_specs(heads, per, biases):
    lane_tile = pl.BlockSpec((1, TOKENS, 128), lambda g, w: (w, 0, g))
    far = pl.BlockSpec((1, WT, 128), lambda g, w: (w, 0, 0))
    bias = [pl.BlockSpec((per,) + b[1:], lambda g, w: (g, 0, 0)) for b in biases]
    exps = [
        pl.BlockSpec((1, 1, KIND_ROWS[i], per * KIND_LANES[i]), lambda g, w: (w, g, 0, 0)) for i in range(3)
    ]
    return lane_tile, far, bias, exps


def exps_shapes(groups, per):
    return [jax.ShapeDtypeStruct((2, groups, KIND_ROWS[i], per * KIND_LANES[i]), BF16) for i in range(3)]


def attend(q, k, v, far, biases, dim):
    width = q.shape[-1]
    heads = width // dim
    per = 128 // dim
    groups = heads // per
    lane_tile, far_spec, bias_specs, exps_specs = head_group_specs(heads, per, [b.shape for b in biases])
    return pl.pallas_call(
        functools.partial(attend_kernel, dim),
        grid=(groups, 2),
        in_specs=[lane_tile] * 3 + [far_spec] + bias_specs,
        out_specs=exps_specs + [lane_tile, lane_tile],
        out_shape=exps_shapes(groups, per)
        + [jax.ShapeDtypeStruct((2, TOKENS, width), BF16), jax.ShapeDtypeStruct((2, TOKENS, width), F32)],
        scratch_shapes=[pltpu.VMEM((RECT[0].count, RECT[0].lanes), F32)],
        compiler_params=pltpu.CompilerParams(vmem_limit_bytes=60 << 20),
        name="attention",
    )(q, k, v, far, *biases)


def attend_back_kernel(
    dim,
    scale,
    q_ref,
    k_ref,
    v_ref,
    g_ref,
    o_ref,
    e0_ref,
    e1_ref,
    e2_ref,
    dq_ref,
    dk_ref,
    dv_ref,
    rows_ref,
    cols_ref,
    a0,
    a1,
    a2,
    a3,
    grads,
    queries,
    outgrads,
):
    win = pl.program_id(1)
    accs = (a0, a1, a2, a3)
    e_refs = (e0_ref, e1_ref, e2_ref)
    per = 128 // dim
    lane = lax.broadcasted_iota(jnp.int32, (16, 128), 1)

    @pl.when(win == 0)
    def _():
        for acc in accs:
            acc[...] = jnp.zeros_like(acc)

    for rect in RECT:
        count, rows, lanes, start = rect.count, rect.rows, rect.lanes, rect.start
        kind_rows = slice(rect.kind_row, rect.kind_row + rows)
        e_ref = e_refs[rect.kind]
        keys = k_ref[0, start : start + rows, :]
        values = v_ref[0, start : start + rows, :]
        out_grad = g_ref[0, start : start + rows, :]
        if lanes > rows:
            out_grad = jnp.concatenate([out_grad, jnp.zeros((lanes - rows, 128), BF16)], axis=0)
        query = q_ref[0, start : start + lanes, :]
        out_grad_t = out_grad.T
        out_t = o_ref[0, start : start + lanes, :].T
        keys_t = keys.T
        product = out_grad_t.astype(F32) * out_t.astype(F32)
        dqs = []
        for head in range(per):
            here = slice(head * lanes, head * lanes + lanes)
            mine = ((lane[:1] >= head * dim) & (lane[:1] < head * dim + dim)).astype(BF16)
            queries[here, :] = query * mine
            outgrads[here, :] = out_grad * mine
            inner = jnp.sum(product[head * dim : head * dim + dim], axis=0, keepdims=True)
            prob_grad = nn(values, head_rows(out_grad_t, head, dim))
            exps = e_ref[0, 0, kind_rows, here].astype(F32)
            score_grad = exps * (prob_grad - inner)
            low = score_grad.astype(BF16)
            accs[rect.table][head, :count, :lanes] += score_grad[:count]
            grads[:rows, here] = low
            dqs.append(nn(keys_t[head * dim : head * dim + dim], low))
        dq = jnp.concatenate(dqs, axis=0) * scale
        dq_ref[0, start : start + rows, :] = dq.T[:rows].astype(BF16)
        dk = nn(grads[:rows, : per * lanes], queries[: per * lanes, :])
        dk_ref[0, start : start + rows, :] = (dk * LN2).astype(BF16)
        dv = nn(e_ref[0, 0, kind_rows, :], outgrads[: per * lanes, :])
        dv_ref[0, start : start + rows, :] = dv.astype(BF16)

    @pl.when(win == 1)
    def _():
        lane8 = lax.broadcasted_iota(jnp.int32, (WT, 128), 1)
        for head in range(per):
            by_rows = [jnp.zeros((WT, 128), F32) for _ in range(ACROSS)]
            by_cols = [jnp.zeros((WT, 128), F32) for _ in range(ACROSS)]
            for acc, totals, (outer, inner) in zip(accs, (by_rows, by_cols, by_rows, by_rows), BIAS_DIMS):
                fold_table(
                    lambda row, tile: acc[head, row : row + WT, tile * 128 : tile * 128 + 128],
                    outer,
                    inner,
                    totals,
                    lane8,
                )
            for d in range(ACROSS):
                rows_ref[head, d] = by_rows[d]
                cols_ref[head, d] = by_cols[d]


def attend_back(q, k, v, out_grad, out, exps, dim):
    width = q.shape[-1]
    heads = width // dim
    per = 128 // dim
    groups = heads // per
    shapes = bias_shapes(heads)
    lane_tile, _, _, exps_specs = head_group_specs(heads, per, shapes)
    strip = pl.BlockSpec((per, ACROSS, WT, 128), lambda g, w: (g, 0, 0, 0))
    strip_shape = jax.ShapeDtypeStruct((heads, ACROSS, WT, 128), F32)
    grad = jax.ShapeDtypeStruct((2, TOKENS, width), BF16)
    most = per * RECT[0].lanes
    return pl.pallas_call(
        functools.partial(attend_back_kernel, dim, dim**-0.5),
        grid=(groups, 2),
        in_specs=[lane_tile] * 5 + exps_specs,
        out_specs=[lane_tile] * 3 + [strip] * 2,
        out_shape=[grad] * 3 + [strip_shape] * 2,
        scratch_shapes=[pltpu.VMEM((per,) + s[1:], F32) for s in shapes]
        + [
            pltpu.VMEM((RECT[0].rows, most), BF16),
            pltpu.VMEM((most, 128), BF16),
            pltpu.VMEM((most, 128), BF16),
        ],
        compiler_params=pltpu.CompilerParams(vmem_limit_bytes=60 << 20),
        name="attention_back",
    )(q, k, v, out_grad, out, *exps)


ERFC = (0.254829592, -0.284496736, 1.421413741, -1.453152027, 1.061405429)
ERFC_P = 0.3275911


def gelu_both(u):
    t = 1.0 / (1.0 + (ERFC_P * 0.5**0.5) * jnp.abs(u))
    bell = jnp.exp2((u * u) * (-0.5 * LOG2E))
    series = 0.5 * ERFC[4]
    for factor in ERFC[3::-1]:
        series = series * t + 0.5 * factor
    tail = series * t * bell
    area = jnp.where(u >= 0.0, 1.0 - tail, tail)
    return u * area, area + u * (bell * (1.0 / np.sqrt(2.0 * np.pi)))


def norm_stats(values):
    centre = values - jnp.mean(values, axis=-1, keepdims=True)
    spread = jnp.mean(centre * centre, axis=-1, keepdims=True)
    inverse = lax.rsqrt(spread + EPS)
    return centre * inverse, inverse


def norm_back(scaled, unit, inverse):
    first = jnp.mean(scaled, axis=-1, keepdims=True)
    second = jnp.mean(scaled * unit, axis=-1, keepdims=True)
    return (scaled - first - unit * second) * inverse


def mlp_kernel(
    tile,
    steps,
    chunk,
    x_ref,
    att_ref,
    r_ref,
    own_ref,
    recv_ref,
    da_ref,
    dm_ref,
    wp_ref,
    pb_ref,
    g_ref,
    b_ref,
    w1_ref,
    b1_ref,
    w2_ref,
    b2_ref,
    mine_ref,
    other_ref,
    mg_ref,
    og_ref,
    gp_ref,
    gw1_ref,
    gw2_ref,
    small_ref,
    fc1b_ref,
    grid32,
    tokens,
    acc_p,
    acc_1,
    acc_2,
    result,
    n2g,
):
    win, step = pl.program_id(0), pl.program_id(1)
    width = x_ref.shape[-1]

    @pl.when((win == 0) & (step == 0))
    def _():
        acc_p[...] = jnp.zeros_like(acc_p)
        acc_1[...] = jnp.zeros_like(acc_1)
        acc_2[...] = jnp.zeros_like(acc_2)
        small_ref[...] = jnp.zeros_like(small_ref)
        fc1b_ref[...] = jnp.zeros_like(fc1b_ref)

    @pl.when(step == 0)
    def _():
        gather_tokens(own_ref.at[0], win * SHIFT_T, grid32)
        gather_tokens(recv_ref.at[0], SHIFT_T - win * SHIFT_T, grid32)
        grid_to_tokens(grid32, tokens)

    here = pl.ds(pl.multiple_of(step * tile, 16), tile)
    da, dm = da_ref[0], dm_ref[0]
    attended = att_ref[0]
    branch = nn(attended, wp_ref[...]) + pb_ref[...]
    middle = x_ref[0].astype(F32) + by_frame(branch, da)
    unit, inverse = norm_stats(middle)
    normed = (unit * g_ref[...] + b_ref[...]).astype(BF16)
    upstream = tokens[here, :]
    result_grad = by_frame(upstream, dm).astype(BF16)
    small_ref[0] += column_sums(result_grad.astype(F32))
    normed_t = normed.T
    result_grad_t = result_grad.T
    for at in range(0, w1_ref.shape[1], chunk):
        part = slice(at, at + chunk)
        hidden = nn(normed, w1_ref[:, part]) + b1_ref[:, part]
        active, slope = gelu_both(hidden)
        active = active.astype(BF16)
        forward = nn(active, w2_ref[part, :])
        acc_2[:, part] += nn(result_grad_t, active)
        hidden_grad = (nt(result_grad, w2_ref[part, :]) * slope).astype(BF16)
        fc1b_ref[:, part] += column_sums(hidden_grad.astype(F32))
        acc_1[:, part] += nn(normed_t, hidden_grad)
        backward = nt(hidden_grad, w1_ref[:, part])
        if at == 0:
            result[...] = forward
            n2g[...] = backward
        else:
            result[...] += forward
            n2g[...] += backward
    tokens[here, :] = middle + by_frame(result[...] + b2_ref[...], dm)
    normed_grad = n2g[...]
    small_ref[1] += column_sums(normed_grad * unit)
    small_ref[2] += column_sums(normed_grad)
    middle_grad = upstream + norm_back(normed_grad * g_ref[...], unit, inverse)
    mg_ref[0] = middle_grad
    branch_grad = by_frame(middle_grad, da).astype(BF16)
    small_ref[3] += column_sums(branch_grad.astype(F32))
    acc_p[...] += nn(attended.T, branch_grad)
    out_grad = nt(branch_grad, wp_ref[...]).astype(BF16)
    og_ref[0] = (out_grad.astype(F32) * r_ref[0]).astype(BF16)

    @pl.when(step == steps - 1)
    def _():
        tokens_to_grid(tokens, grid32)
        grid_to_frames(grid32, win * SHIFT_T, mine_ref.at[0])
        grid_to_frames(grid32, SHIFT_T - win * SHIFT_T, other_ref.at[0])

    @pl.when((win == 1) & (step == steps - 1))
    def _():
        gp_ref[...] = acc_p[...].astype(BF16)
        gw1_ref[...] = acc_1[...].astype(BF16)
        gw2_ref[...] = acc_2[...].astype(BF16)


def mlp(x, att, inverse, cot, cot_recv, drop_attn, drop_mlp, wp, pb, g, b, w1, b1, w2, b2, tile=400, chunk=512):
    width, hidden = w1.shape
    steps = TOKENS // tile
    frames = pl.BlockSpec((1, WT, 128), lambda w, j: (w, 0, 0))
    return pl.pallas_call(
        functools.partial(mlp_kernel, tile, steps, chunk),
        grid=(2, steps),
        in_specs=[
            tile_spec(tile, width),
            tile_spec(tile, width),
            tile_spec(tile, width),
            half_spec(SIDE, width),
            other_spec(SIDE, width),
            frames,
            frames,
            whole(wp.shape),
            whole((1, width)),
            whole((1, width)),
            whole((1, width)),
            whole(w1.shape),
            whole((1, hidden)),
            whole(w2.shape),
            whole((1, width)),
        ],
        out_specs=[
            half_spec(SIDE, width),
            other_spec(SIDE, width),
            tile_spec(tile, width),
            tile_spec(tile, width),
            whole((width, width)),
            whole((width, hidden)),
            whole((width, hidden)),
            whole((4, 8, width)),
            whole((8, hidden)),
        ],
        out_shape=[
            jax.ShapeDtypeStruct(cot.shape, BF16),
            jax.ShapeDtypeStruct(cot_recv.shape, BF16),
            jax.ShapeDtypeStruct((2, TOKENS, width), F32),
            jax.ShapeDtypeStruct((2, TOKENS, width), BF16),
            jax.ShapeDtypeStruct((width, width), BF16),
            jax.ShapeDtypeStruct((width, hidden), BF16),
            jax.ShapeDtypeStruct((width, hidden), BF16),
            jax.ShapeDtypeStruct((4, 8, width), F32),
            jax.ShapeDtypeStruct((8, hidden), F32),
        ],
        scratch_shapes=[
            pltpu.VMEM((4, WT * FRAME_ROWS, 128), F32),
            pltpu.VMEM((TOKENS, width), F32),
            pltpu.VMEM((width, width), F32),
            pltpu.VMEM((width, hidden), F32),
            pltpu.VMEM((width, hidden), F32),
            pltpu.VMEM((tile, width), F32),
            pltpu.VMEM((tile, width), F32),
        ],
        compiler_params=pltpu.CompilerParams(vmem_limit_bytes=62 << 20),
        name="mlp",
    )(x, att, inverse, cot, cot_recv, drop_attn, drop_mlp, wp, pb[None], g[None], b[None], w1, b1[None], w2, b2[None])


def qkv_back_kernel(
    tile,
    steps,
    dq_ref,
    dk_ref,
    dv_ref,
    n_ref,
    x_ref,
    mg_ref,
    w_ref,
    g_ref,
    mine_ref,
    other_ref,
    gw_ref,
    small_ref,
    grid32,
    tokens,
    acc,
):
    win, step = pl.program_id(0), pl.program_id(1)
    width = x_ref.shape[-1]

    @pl.when((win == 0) & (step == 0))
    def _():
        acc[...] = jnp.zeros_like(acc)
        small_ref[...] = jnp.zeros_like(small_ref)

    here = pl.ds(pl.multiple_of(step * tile, 16), tile)
    dq, dk, dv = dq_ref[0], dk_ref[0], dv_ref[0]
    normed_t = n_ref[0].T
    acc[:, :width] += nn(normed_t, dq)
    acc[:, width : 2 * width] += nn(normed_t, dk)
    acc[:, 2 * width :] += nn(normed_t, dv)
    small_ref[0] += column_sums(dq.astype(F32))
    small_ref[1] += column_sums(dv.astype(F32))
    normed_grad = (
        nt(dq, w_ref[:, :width]) + nt(dk, w_ref[:, width : 2 * width]) + nt(dv, w_ref[:, 2 * width :])
    )
    unit, inverse = norm_stats(x_ref[0].astype(F32))
    small_ref[2] += column_sums(normed_grad * unit)
    small_ref[3] += column_sums(normed_grad)
    tokens[here, :] = mg_ref[0] + norm_back(normed_grad * g_ref[...], unit, inverse)

    @pl.when(step == steps - 1)
    def _():
        tokens_to_grid(tokens, grid32)
        grid_to_frames(grid32, win * SHIFT_T, mine_ref.at[0])
        grid_to_frames(grid32, SHIFT_T - win * SHIFT_T, other_ref.at[0])

    @pl.when((win == 1) & (step == steps - 1))
    def _():
        gw_ref[...] = acc[...].astype(BF16)


def qkv_back(dq, dk, dv, normed, x, middle_grad, w_qkv, gain, tile=400):
    width = x.shape[-1]
    steps = TOKENS // tile
    return pl.pallas_call(
        functools.partial(qkv_back_kernel, tile, steps),
        grid=(2, steps),
        in_specs=[tile_spec(tile, width)] * 6 + [whole(w_qkv.shape), whole((1, width))],
        out_specs=[
            half_spec(SIDE, width),
            other_spec(SIDE, width),
            whole(w_qkv.shape),
            whole((4, 8, width)),
        ],
        out_shape=[
            jax.ShapeDtypeStruct((2, 2 * SHIFT_T, SIDE, SIDE, width), F32),
            jax.ShapeDtypeStruct((2, SHIFT_T, SIDE, SIDE, width), BF16),
            jax.ShapeDtypeStruct(w_qkv.shape, BF16),
            jax.ShapeDtypeStruct((4, 8, width), F32),
        ],
        scratch_shapes=[
            pltpu.VMEM((4, WT * FRAME_ROWS, 128), F32),
            pltpu.VMEM((TOKENS, width), F32),
            pltpu.VMEM(w_qkv.shape, F32),
        ],
        compiler_params=pltpu.CompilerParams(vmem_limit_bytes=60 << 20),
        name="qkv_back",
    )(dq, dk, dv, normed, x, middle_grad, w_qkv, gain[None])


def neighbours():
    count = lax.axis_size("tm")
    down = [(i, i - 1) for i in range(1, count)]
    up = [(i, i + 1) for i in range(count - 1)]
    return count, down, up


def fetch_halves(field):
    count, down, up = neighbours()
    me = lax.axis_index("tm")
    above = lax.ppermute(field[0, :SHIFT_T], "tm", down)
    below = lax.ppermute(field[1, SHIFT_T:], "tm", up)
    above = jnp.where(me == count - 1, field[1, SHIFT_T:], above)
    below = jnp.where(me == 0, field[0, :SHIFT_T], below)
    return jnp.stack([above, below])


def return_halves(mine, other):
    count, down, up = neighbours()
    me = lax.axis_index("tm")
    from_below = lax.ppermute(other[0], "tm", up)
    from_above = lax.ppermute(other[1], "tm", down)
    first = jnp.where(me == 0, other[1], from_below).astype(mine.dtype)
    last = jnp.where(me == count - 1, other[0], from_above).astype(mine.dtype)
    mine = lax.dynamic_update_slice(mine, first[None], (0, 0, 0, 0, 0))
    return lax.dynamic_update_slice(mine, last[None], (1, SHIFT_T, 0, 0, 0))


def frame_facts(segments, keep):
    count = lax.axis_size("tm")
    me = lax.axis_index("tm")
    own = 2 * SHIFT_T
    first = me * own
    t = jnp.arange(SHIFT_T)
    zero, one = jnp.zeros((SHIFT_T,), jnp.int32), jnp.ones((SHIFT_T,), jnp.int32)
    top, bottom = me == count - 1, me == 0
    frames = jnp.stack(
        [
            jnp.concatenate([first + SHIFT_T + t, jnp.where(top, first + SHIFT_T + t, first + own + t)]),
            jnp.concatenate([jnp.where(bottom, t, first - SHIFT_T + t), first + t]),
        ]
    )
    volumes = jnp.stack(
        [jnp.concatenate([zero, jnp.where(top, one, zero)]), jnp.concatenate([jnp.where(bottom, zero, one), one])]
    )
    pick = (frames[:, :, None] == jnp.arange(segments.shape[1])).astype(jnp.int32)
    by_volume = jnp.sum(pick[:, :, None, :] * segments[None, None], axis=-1)
    segment = jnp.where(volumes == 0, by_volume[..., 0], by_volume[..., 1])
    key = segment + 8 * (frames < SHIFT_T) + 16 * volumes
    apart = (key[:, :, None] != key[:, None, :]).astype(F32) * FAR
    far = jnp.tile(apart, (1, 1, 128 // WT))
    seg_hot = (segment[:, :, None] == jnp.arange(keep.shape[2])).astype(F32)
    kept = jnp.where(volumes[:, :, None, None] == 0, keep[0], keep[1]).astype(F32)
    drops = jnp.sum(seg_hot[:, :, None, :] * kept, axis=-1) / KEEP_RATE
    drops = jnp.broadcast_to(drops[..., None], drops.shape + (128,))
    return far, drops[:, :, 0], drops[:, :, 1]


def shards(
    volume,
    segments,
    keep,
    ln1_gain,
    ln1_bias,
    w_qkv,
    q_bias,
    v_bias,
    rel_table,
    w_proj,
    proj_bias,
    ln2_gain,
    ln2_bias,
    w_fc1,
    fc1_bias,
    w_fc2,
    fc2_bias,
    cotangent,
):
    width = volume.shape[-1]
    heads = rel_table.shape[1]
    dim = width // heads
    recv = fetch_halves(volume)
    cot_recv = fetch_halves(cotangent)
    far, drop_attn, drop_mlp = frame_facts(segments, keep)
    biases = make_bias(rel_table)
    qkv_bias = jnp.concatenate([q_bias, jnp.zeros_like(q_bias), v_bias])
    x, normed, q, k, v = make_qkv(volume, recv, ln1_gain, ln1_bias, w_qkv, qkv_bias, dim**-0.5 * LOG2E)
    *exps, att, inverse = attend(q, k, v, far, biases, dim)
    mixed, mixed_other, middle_grad, out_grad, g_proj, g_fc1, g_fc2, small2, small_fc1 = mlp(
        x,
        att,
        inverse,
        cotangent,
        cot_recv,
        drop_attn,
        drop_mlp,
        w_proj,
        proj_bias,
        ln2_gain,
        ln2_bias,
        w_fc1,
        fc1_bias,
        w_fc2,
        fc2_bias,
    )
    mixed_out = return_halves(mixed, mixed_other)
    g_proj, g_fc1, g_fc2 = lax.psum((g_proj, g_fc1, g_fc2), ("dp", "tm"))
    dq, dk, dv, by_rows, by_cols = attend_back(q, k, v, out_grad, att, exps, dim)
    grad, grad_other, g_qkv, small1 = qkv_back(dq, dk, dv, normed, x, middle_grad, w_qkv, ln1_gain)
    volume_grad = return_halves(grad, grad_other)
    shape = (heads, ACROSS, WT, 128)
    by_rows = by_rows.reshape(shape)[..., : ACROSS * WT].reshape(heads, ACROSS, WT, ACROSS, WT)
    by_cols = by_cols.reshape(shape)[..., : ACROSS * WT].reshape(heads, ACROSS, WT, ACROSS, WT)
    table = jnp.einsum("nakbs,ksd->dabn", by_rows, time_hot(), precision=PRECISE) + jnp.einsum(
        "nbkas,ksd->dabn", by_cols, time_hot(), precision=PRECISE
    )
    vectors = jnp.concatenate(
        [
            jnp.sum(small2, axis=1).reshape(-1),
            jnp.sum(small_fc1, axis=0).reshape(-1),
            jnp.sum(small1, axis=1).reshape(-1),
            table.reshape(-1),
        ]
    )
    g_qkv, vectors = lax.psum((g_qkv, vectors), ("dp", "tm"))
    hidden = w_fc1.shape[1]
    small2 = vectors[: 4 * width].reshape(4, width)
    fc1_b = vectors[4 * width : 4 * width + hidden]
    small1 = vectors[4 * width + hidden : 8 * width + hidden].reshape(4, width)
    table = vectors[8 * width + hidden :].reshape(rel_table.shape)
    return (
        mixed_out,
        volume_grad,
        small1[2],
        small1[3],
        g_qkv.astype(F32),
        small1[0],
        small1[1],
        table,
        g_proj.astype(F32),
        small2[3],
        small2[1],
        small2[2],
        g_fc1.astype(F32),
        fc1_b,
        g_fc2.T.astype(F32),
        small2[0],
    )


def solution(mesh):
    split = P("dp", "tm", None, None, None)
    return jax.shard_map(
        shards,
        mesh=mesh,
        in_specs=(split, P("dp", None), P("dp", None, None)) + (P(),) * 14 + (split,),
        out_specs=(split, split) + (P(),) * 14,
        check_vma=False,
    )
```

time: 2390 us -> 714 us (0.30)
  local copies, waits for them, and re-layouts: 1130 us -> 84.5 us
  matrix products: 661 us -> 25 us
  other arithmetic: 364 us -> 25.3 us
  Pallas kernels: 0 us -> 284 us
  waiting for transfers between devices: 147 us -> 255 us
  blocking collectives: 39.5 us -> 0 us
    dot_general x46 -> x3, matrix products: 661 us -> 25 us  [the longest x1 11.5 us: shards(): jnp.einsum('nbkas,ksd->dabn', by_cols, time_hot(), precision=PRECISE)]
    add x14 -> x1, local copies, waits for them, and re-layouts: 607 us -> 1.74 us  [shards(): jnp.einsum('nakbs,ksd->dabn', by_rows, time_hot(), precision=PRECISE)]
    pallas_call x0 -> x6, Pallas kernels: none -> 284 us  [the longest x1 96.1 us: mlp(): pl.pallas_call(functools.partial(mlp_kernel, tile, steps, chunk), grid=(2...]
    reduce_sum x17 -> x5, other arithmetic: 197 us -> 1.23 us  [the longest x1 0.87 us: shards(): jnp.sum(small1, axis=1).reshape(-1)]
    while x11 -> x0, local copies, waits for them, and re-layouts: 133 us -> none  [the longest x2 86.8 us: shards(): attended_win, log_totals = lax.map(forward_block, (blocks, combos))]
    psum x1 -> x2, waiting for transfers between devices: 128 us -> 238 us  [the longest x1 127 us: shards(): g_proj, g_fc1, g_fc2 = lax.psum((g_proj, g_fc1, g_fc2), ('dp', 'tm'))]
    reshape x4 -> x6, local copies, waits for them, and re-layouts: 93.1 us -> 14.8 us  [the longest x2 7.03 us: make_bias(): by_rows = jnp.pad(both.reshape(heads, ACROSS, WT, ACROSS * WT), pad)]
    dynamic_update_slice x16 -> x0, local copies, waits for them, and re-layouts: 70 us -> none  [the longest x8 53.3 us: shards(): lax.scan(backward_block, jnp.zeros((head_count, wtok, wtok), jnp.float32)...]
  transfers between devices with their start and end apart: 5 -> 10, of which waited for: 2 -> 3; matrix products, arithmetic and copies ran while one was open for 21% -> 11% of each run, Pallas kernels for 0% -> 1%
where the time goes in v1:
time: 714 us; the launch traced here: 713 us
  Pallas kernels  284 us (40%)
  waiting for transfers between devices  255 us (36%)
  local copies, waits for them, and re-layouts  84.5 us (12%)
  other arithmetic  25.3 us (4%)
  matrix products  25 us (4%)
  starting transfers between devices  24.4 us (3%)
  between operations  14.8 us (2%)
    psum x1, waiting for transfers between devices, shards(): g_proj, g_fc1, g_fc2 = lax.psum((g_proj, g_fc1, g_fc2), ('dp', 'tm'))  127 us
    psum x1, waiting for transfers between devices, shards(): g_qkv, vectors = lax.psum((g_qkv, vectors), ('dp', 'tm'))  111 us
    pallas_call x1, Pallas kernels, mlp(): pl.pallas_call(functools.partial(mlp_kernel, tile, steps, chunk), grid=(2...  96.1 us
    pallas_call x1, Pallas kernels, attend_back(): pl.pallas_call(functools.partial(attend_back_kernel, dim, dim ** (-0.5)),...  77.3 us
    pallas_call x1, Pallas kernels, attend(): pl.pallas_call(functools.partial(attend_kernel, dim), grid=(groups, 2), i...  55.4 us
    pallas_call x1, Pallas kernels, qkv_back(): pl.pallas_call(functools.partial(qkv_back_kernel, tile, steps), grid=(2,...  28.2 us
    unnamed x52, local copies, waits for them, and re-layouts  25.7 us
    pallas_call x1, Pallas kernels, make_qkv(): pl.pallas_call(functools.partial(qkv_kernel, tile, scale), grid=(2, TOKEN...  17.1 us
  transfers between devices with their start and end apart: 10, of which 3 were waited for; matrix products, arithmetic and copies ran while one was open for 11% of the time, Pallas kernels for 1%

profile of v1, /device:TPU:0, one launch (start us, length us, event | category | flops | bytes accessed | tf_op | source)
XLA Modules:
  0.0 713.1 jit_solution(17370006597111701806)
XLA Ops:
  7.2 3.1 copy.116.own_ref
  12.2 6.0 collective-permute-start.1
  24.4 5.5 collective-permute-start.3
  33.7 13.2 %copy.146 = f32[15,13,13,16,1]{3,0,4,2,1:T(8,128)S(1)} copy(f32[15,13,13,16,1]{2,1,0,3,4:T(8,128)S(1)} %bitcast.139) | data formatting | bytes 324480 | tf_op jit(solution)/shard_map/mul | solution.py:203
  47.0 4.6 fusion.30
  51.6 2.8 copy_bitcast_fusion
  54.4 2.9 copy_bitcast_fusion.1
  59.2 4.2 copy.121
  63.4 4.2 copy.119
  67.6 10.1 %position_bias.1 = (f32[16,392,512]{2,1,0:T(8,128)}, f32[16,224,256]{2,1,0:T(8,128)}, f32[16,128,128]{2,1,0:T(8,128)S(1)}, f32[16,96,128]{2,1,0:T(8,128)S(1)}) custom-call(f32[16,13,8,128]{3,2,1,0:T(8,128)S(1)} %pad.9.rows_ref, f32[16,13,8,128]{3,2,1,0:T(8,128)S(1)} %pad.10.cols_ref), custom_call_target="tpu_custom_call" | custom-call | tf_op jit(solution)/shard_map/position_bias/pallas_call | solution.py:211
  78.0 4.6 fusion.14
  85.6 17.1 %norm1_qkv.1 = (bf16[2,1600,512]{2,1,0:T(8,128)(2,1)}, bf16[2,1600,512]{2,1,0:T(8,128)(2,1)}, bf16[2,1600,512]{2,1,0:T(8,128)(2,1)}, bf16[2,1600,512]{2,1,0:T(8,128)(2,1)}, bf16[2,1600,512]{2,1,0:T(8,128)(2,1)}) custom-call(bf16[2,8,14,14,512]{4,3,2,1,0:T(8,128)(2,1)} %copy-done.2, bf16[2,4,14,14,512]{4,3,2,1,0:T(8,128)(2,1)} %pad_maximum_fusion.recv_ref, ...), custom_call_target="tpu_custom_call" | custom-call | tf_op jit(solution)/shard_map/norm1_qkv/pallas_call | solution.py:285
  102.7 55.4 %attention.1 = (bf16[2,4,400,2048]{3,2,1,0:T(8,128)(2,1)}, bf16[2,4,800,1024]{3,2,1,0:T(8,128)(2,1)}, bf16[2,4,400,512]{3,2,1,0:T(8,128)(2,1)}, bf16[2,1600,512]{2,1,0:T(8,128)(2,1)}, f32[2,1600,512]{2,1,0:T(8,128)}) custom-call(bf16[2,1600,512]{2,1,0:T(8,128)(2,1)} %get-tuple-element.49.q_ref, bf16[2,1600,512]{2,1,0:T(8,128)(2,1)} %get-tuple-element.50.k_ref, ...), custom_call_target="tpu_custom_call" | custom-call | tf_op jit(solution)/shard_map/attention/pallas_call | solution.py:376
  159.4 96.1 %mlp.1 = (bf16[2,8,14,14,512]{4,3,2,1,0:T(8,128)(2,1)}, bf16[2,4,14,14,512]{4,3,2,1,0:T(8,128)(2,1)}, f32[2,1600,512]{2,1,0:T(8,128)}, bf16[2,1600,512]{2,1,0:T(...) custom-call(bf16[2,1600,512]{2,1,0:T(8,128)(2,1)} %get-tuple-element, ...), custom_call_target="tpu_custom_call" | custom-call | tf_op jit(solution)/shard_map/mlp/pallas_call | solution.py:645
  255.5 77.3 %attention_back.1 = (bf16[2,1600,512]{2,1,0:T(8,128)(2,1)}, bf16[2,1600,512]{2,1,0:T(8,128)(2,1)}, bf16[2,1600,512]{2,1,0:T(8,128)(2,1)}, f32[16,13,8,128]{3,2,1,0:T(8,128)}, f32[16,13,8,128]{3,2,1,0:T(8,128)}) custom-call(bf16[2,1600,512]{2,1,0:T(8,128)(2,1)} %get-tuple-element.49.q_ref, bf16[2,1600,512]{2,1,0:T(8,128)(2,1)} %get-tuple-element.50.k_ref, ...), custom_call_target="tpu_custom_call" | custom-call | tf_op jit(solution)/shard_map/attention_back/pallas_call | solution.py:489
  332.8 28.2 %qkv_back.1 = (f32[2,8,14,14,512]{4,3,2,1,0:T(8,128)}, bf16[2,4,14,14,512]{4,3,2,1,0:T(8,128)(2,1)}, bf16[512,1536]{1,0:T(8,128)(2,1)}, f32[4,8,512]{2,1,0:T(8,128)}) custom-call(bf16[2,1600,512]{2,1,0:T(8,128)(2,1)} %get-tuple-element.64.dq_ref, bf16[2,1600,512]{2,1,0:T(8,128)(2,1)} %get-tuple-element.65.dk_ref, ...), custom_call_target="tpu_custom_call" | custom-call | tf_op jit(solution)/shard_map/qkv_back/pallas_call | solution.py:758
  362.0 3.9 copy.137
  365.9 4.1 copy.139
  370.0 11.5 %fusion.4 = f32[15,13,13,16]{0,3,2,1:T(8,128)S(1)} fusion(f32[8,8,15,1,1]{2,1,0,3,4:T(8,128)S(1)} %copy-done.17, f32[16,13,8,104]{0,3,2,1:T(8,128)} %copy.139), kind=kOutput, calls=%fused_computation.10 | convolution fusion | flops 31150080 | bytes 858304 | tf_op jit(solution)/shard_map/nbkas,ksd->dabn/dot_general | solution.py:897
  381.6 8.8 %fusion.10 = f32[15,13,13,16]{0,3,2,1:T(8,128)S(1)} fusion(f32[15,13,13,16]{0,3,2,1:T(8,128)S(1)} %fusion.4, f32[16,13,8,104]{0,3,2,1:T(8,128)S(1)} %copy-done.4, f32[8,8,15,1,1]{2,1,0,4,3:T(8,128)S(1)} %copy-done.14), kind=kOutput, calls=%fused_computation.12 | convolution fusion | flops 31190640 | bytes 1020544 | tf_op jit(solution)/shard_map/nakbs,ksd->dabn/dot_general | solution.py:897
  397.0 5.4 collective-permute-start.4
  404.1 2.2 collective-permute-start.6
  409.1 110.6 %all-reduce.8.cloned.1.call-done = f32[46704]{0:T(1024)} async-done(((f32[46704]{0:T(1024)}), f32[46704]{0:T(1024)}) %all-reduce.8.cloned.1.call-update) | async-done | bytes 186832 | tf_op jit(solution)/shard_map/psum | solution.py:908
  523.4 2.7 slice_bitcast_fusion.7
  529.4 2.7 convert_dynamic-update-slice_fusion.1
  532.2 2.9 convert_dynamic-update-slice_fusion
  535.1 12.0 %copy.143 = f32[2,8,14,14,512]{4,1,3,2,0:T(8,128)} copy(f32[2,8,14,14,512]{4,3,2,1,0:T(8,128)} %convert_dynamic-update-slice_fusion) | data formatting | bytes 12845056
  547.1 16.5 %collective-permute-done.5 = bf16[4,14,14,512]{3,0,2,1:T(4,128)(2,1)S(1)} collective-permute-done((bf16[4,14,14,512]{3,0,2,1:T(4,128)(2,1)S(1)}, bf16[4,14,14,512]{3,0,2,1:T(4,128)(2,1)S(1)}, u32[]{:S(2)}, u32[]{:S(2)}) %collective-permute-start.5) | collective-permute-done | bytes 802848 | tf_op jit(solution)/shard_map/ppermute | solution.py:805
  563.9 3.9 copy.142
  567.9 127.2 %all-reduce.10.cloned.1.call-done = (bf16[2048,512]{0,1:T(8,128)(2,1)}, bf16[512,1536]{1,0:T(8,128)(2,1)}, bf16[512,512]{1,0:T(8,128)(2,1)}, bf16[512,2048]{1,0:T(8,128)(2,1)}) async-done(((bf16[2048,512]{0,1:T(8,128)(2,1)}, bf16[512,1536]{1,0:T(8,128)(2,1)}, bf16[512,512]{1,0:T(8,128)(2,1)}, bf16[512,2048]{1,0:T(8,128)(2,1)}), (bf16[2048,512]{0,1:T(8,128)(2,1)}, bf16[512,1536]{1,0:T(8,128)(2,1)}, ...) | async-done | bytes 6291472 | tf_op jit(solution)/shard_map/psum | solution.py:890
  697.2 4.2 copy.145
  703.5 2.5 convert_element_type.44
  (121 shorter events, 41.8 us)
Async XLA Ops:
  7.2 512.5 %all-reduce.8.cloned.1.call-start = ((), (), s32[]{:S(2)}) async-start(), calls=%async_computation | async-start | bytes 376832 | tf_op jit(solution)/shard_map/psum | solution.py:908
  10.3 9.4 %copy-start.2 = (bf16[2,8,14,14,512]{4,3,2,1,0:T(8,128)(2,1)}, bf16[2,8,14,14,512]{4,3,2,1,0:T(8,128)(2,1)S(1)}, u32[]{:S(2)}) copy-start(bf16[2,8,14,14,512]{4,3,2,1,0:T(8,128)(2,1)S(1)} %copy.116.own_ref) | copy-start | bytes 9633796
  10.4 10.7 %copy-start.8 = (bf16[2,8,14,14,512]{4,1,3,2,0:T(8,128)(2,1)S(1)}, bf16[2,8,14,14,512]{4,1,3,2,0:T(8,128)(2,1)}, u32[]{:S(2)}) copy-start(bf16[2,8,14,14,512]{4,1,3,2,0:T(8,128)(2,1)} %param.39) | copy-start | bytes 9633796
  12.2 65.7 %collective-permute-start.1 = (bf16[4,14,14,512]{3,0,2,1:T(4,128)(2,1)}, bf16[4,14,14,512]{3,0,2,1:T(4,128)(2,1)}, u32[]{:S(2)}, u32[]{:S(2)}) collective-permute-start(bf16[4,14,14,512]{3,0,2,1:T(4,128)(2,1)} %copy.114), channel_id=1, source_target_pairs={{0,1},{1,2},{2,3},{4,5},{5,6},{6,7},{8,9},{9,10},{10,11},{12,13},{... | collective-permute-start | bytes 2408456 | tf_op jit(solution)/shard_map/ppermute | solution.py:795
  19.7 58.2 %collective-permute-start = (bf16[4,14,14,512]{3,0,2,1:T(4,128)(2,1)}, bf16[4,14,14,512]{3,0,2,1:T(4,128)(2,1)}, u32[]{:S(2)}, u32[]{:S(2)}) collective-permute-start(bf16[4,14,14,512]{3,0,2,1:T(4,128)(2,1)} %copy.112), channel_id=1, source_target_pairs={{1,0},{2,1},{3,2},{5,4},{6,5},{7,6},{9,8},{10,9},{11,10},{13,12},{... | collective-permute-start | bytes 2408456 | tf_op jit(solution)/shard_map/ppermute | solution.py:794
  22.3 9.1 %copy-start.3 = (bf16[2,8,14,14,512]{4,3,2,1,0:T(8,128)(2,1)}, bf16[2,8,14,14,512]{4,3,2,1,0:T(8,128)(2,1)S(1)}, u32[]{:S(2)}) copy-start(bf16[2,8,14,14,512]{4,3,2,1,0:T(8,128)(2,1)S(1)} %copy.128.own_ref) | copy-start | bytes 9633796
  22.3 10.5 %copy-start.13 = (f32[2535,16]{0,1:T(8,128)S(1)}, f32[2535,16]{0,1:T(8,128)}, u32[]{:S(2)}) copy-start(f32[2535,16]{0,1:T(8,128)} %param.30) | copy-start | bytes 486724
  24.4 53.6 %collective-permute-start.3 = (bf16[4,14,14,512]{3,0,2,1:T(4,128)(2,1)}, bf16[4,14,14,512]{3,0,2,1:T(4,128)(2,1)}, u32[]{:S(2)}, u32[]{:S(2)}) collective-permute-start(bf16[4,14,14,512]{3,0,2,1:T(4,128)(2,1)} %copy.126), channel_id=1, source_target_pairs={{0,1},{1,2},{2,3},{4,5},{5,6},{6,7},{8,9},{9,10},{10,11},{12,13},{... | collective-permute-start | bytes 2408456 | tf_op jit(solution)/shard_map/ppermute | solution.py:795
  31.4 15.6 %copy-start.14 = (f32[8,8,15,1,1]{2,1,0,4,3:T(8,128)S(1)}, f32[8,8,15,1,1]{2,1,0,4,3:T(8,128)}, u32[]{:S(2)}) copy-start(f32[8,8,15,1,1]{2,1,0,4,3:T(8,128)} %constant.52) | copy-start | bytes 11524
  31.4 46.6 %collective-permute-start.2 = (bf16[4,14,14,512]{3,0,2,1:T(4,128)(2,1)}, bf16[4,14,14,512]{3,0,2,1:T(4,128)(2,1)}, u32[]{:S(2)}, u32[]{:S(2)}) collective-permute-start(bf16[4,14,14,512]{3,0,2,1:T(4,128)(2,1)} %copy.124), channel_id=1, source_target_pairs={{1,0},{2,1},{3,2},{5,4},{6,5},{7,6},{9,8},{10,9},{11,10},{13,12},{... | collective-permute-start | bytes 2408456 | tf_op jit(solution)/shard_map/ppermute | solution.py:794
  54.4 2.9 copy-start.20
  54.4 3.1 copy-start.21
  54.4 3.4 copy-start.18
  54.4 3.4 copy-start.19
  77.7 4.9 copy-start
  77.7 4.9 copy-start.1
  332.8 29.1 %copy-start.16 = (f32[4,8,512]{2,1,0:T(8,128)S(1)}, f32[4,8,512]{2,1,0:T(8,128)}, u32[]{:S(2)}) copy-start(f32[4,8,512]{2,1,0:T(8,128)} %get-tuple-element.71) | copy-start | bytes 196612
  332.8 29.2 %copy-start.15 = (f32[8,2048]{1,0:T(8,128)S(1)}, f32[8,2048]{1,0:T(8,128)}, u32[]{:S(2)}) copy-start(f32[8,2048]{1,0:T(8,128)} %get-tuple-element.72) | copy-start | bytes 196612
  332.8 29.2 %copy-start.12 = (f32[16,13,8,128]{3,2,1,0:T(8,128)S(1)}, f32[16,13,8,128]{3,2,1,0:T(8,128)}, u32[]{:S(2)}) copy-start(f32[16,13,8,128]{3,2,1,0:T(8,128)} %get-tuple-element.74) | copy-start | bytes 2555908
  361.9 4.0 copy-start.11
  365.9 4.1 copy-start.17
  370.0 11.6 %copy-start.4 = (f32[16,13,8,104]{0,3,2,1:T(8,128)S(1)}, f32[16,13,8,104]{0,3,2,1:T(8,128)}, u32[]{:S(2)}) copy-start(f32[16,13,8,104]{0,3,2,1:T(8,128)} %copy.137) | copy-start | bytes 2076676
  393.3 301.7 %all-reduce.10.cloned.1.call-start = ((), (), s32[]{:S(2)}) async-start(), calls=%async_computation.1 | async-start | bytes 12582912 | tf_op jit(solution)/shard_map/psum | solution.py:890
  394.1 8.3 %copy-start.5 = (bf16[2,4,14,14,512]{4,3,2,1,0:T(8,128)(2,1)S(1)}, bf16[2,4,14,14,512]{4,3,2,1,0:T(8,128)(2,1)}, u32[]{:S(2)}) copy-start(bf16[2,4,14,14,512]{4,3,2,1,0:T(8,128)(2,1)} %get-tuple-element.70) | copy-start | bytes 4816900
  397.0 126.4 %collective-permute-start.4 = (bf16[4,14,14,512]{3,0,2,1:T(4,128)(2,1)}, bf16[4,14,14,512]{3,0,2,1:T(4,128)(2,1)}, u32[]{:S(2)}, u32[]{:S(2)}) collective-permute-start(bf16[4,14,14,512]{3,0,2,1:T(4,128)(2,1)} %copy.129), channel_id=1, source_target_pairs={{0,1},{1,2},{2,3},{4,5},{5,6},{6,7},{8,9},{9,10},{10,11},{12,13},{... | collective-permute-start | bytes 2408456 | tf_op jit(solution)/shard_map/ppermute | solution.py:804
  404.1 125.3 %collective-permute-start.6 = (bf16[4,14,14,512]{3,0,2,1:T(4,128)(2,1)}, bf16[4,14,14,512]{3,0,2,1:T(4,128)(2,1)}, u32[]{:S(2)}, u32[]{:S(2)}) collective-permute-start(bf16[4,14,14,512]{3,0,2,1:T(4,128)(2,1)} %copy.133), channel_id=1, source_target_pairs={{0,1},{1,2},{2,3},{4,5},{5,6},{6,7},{8,9},{9,10},{10,11},{12,13},{... | collective-permute-start | bytes 2408456 | tf_op jit(solution)/shard_map/ppermute | solution.py:804
  407.8 124.3 %collective-permute-start.7 = (bf16[4,14,14,512]{3,0,2,1:T(4,128)(2,1)}, bf16[4,14,14,512]{3,0,2,1:T(4,128)(2,1)}, u32[]{:S(2)}, u32[]{:S(2)}) collective-permute-start(bf16[4,14,14,512]{3,0,2,1:T(4,128)(2,1)} %copy.135), channel_id=1, source_target_pairs={{1,0},{2,1},{3,2},{5,4},{6,5},{7,6},{9,8},{10,9},{11,10},{13,12},{... | collective-permute-start | bytes 2408456 | tf_op jit(solution)/shard_map/ppermute | solution.py:805
  526.7 36.8 %collective-permute-start.5 = (bf16[4,14,14,512]{3,0,2,1:T(4,128)(2,1)S(1)}, bf16[4,14,14,512]{3,0,2,1:T(4,128)(2,1)S(1)}, u32[]{:S(2)}, u32[]{:S(2)}) collective-permute-start(bf16[4,14,14,512]{3,0,2,1:T(4,128)(2,1)S(1)} %copy.131), channel_id=1, source_target_pairs={{1,0},{2,1},{3,2},{5,4},{6,5},{7,6},{9,8},{10,9},{11,10},{13,12},{... | collective-permute-start | bytes 2408456 | tf_op jit(solution)/shard_map/ppermute | solution.py:805
  535.1 28.5 %copy-start.6 = (bf16[2,4,14,14,512]{4,3,2,1,0:T(8,128)(2,1)S(1)}, bf16[2,4,14,14,512]{4,3,2,1,0:T(8,128)(2,1)}, u32[]{:S(2)}) copy-start(bf16[2,4,14,14,512]{4,3,2,1,0:T(8,128)(2,1)} %get-tuple-element.59) | copy-start | bytes 4816900
  535.1 28.5 %copy-start.7 = (bf16[2,8,14,14,512]{4,3,2,1,0:T(8,128)(2,1)S(1)}, bf16[2,8,14,14,512]{4,3,2,1,0:T(8,128)(2,1)}, u32[]{:S(2)}) copy-start(bf16[2,8,14,14,512]{4,3,2,1,0:T(8,128)(2,1)} %get-tuple-element.161) | copy-start | bytes 9633796
  697.2 4.2 copy-start.10
  701.5 2.1 copy-start.9
Sparse Core Ops, SparseCore 0:
  393.4 126.2 all-reduce.7
  526.3 168.6 all-reduce.9

commit v2 on v1

v2 whole, which is shorter than its diff:
```python
import functools

import jax
import jax.numpy as jnp
import numpy as np
from jax import lax
from jax.experimental import pallas as pl
from jax.experimental.pallas import tpu as pltpu
from jax.sharding import PartitionSpec as P

SIDE = 14
WT = 8
WIN_HW = 7
SHIFT_T = 4
SHIFT_HW = 3
EPS = 1e-05
KEEP_RATE = 0.75
PRECISE = lax.Precision.HIGHEST
LOG2E = 1.4426950408889634
LN2 = 0.6931471805599453
FAR = 1e30
F32 = jnp.float32
BF16 = jnp.bfloat16

SPANS = (
    (SHIFT_HW, WIN_HW),
    (SHIFT_HW + WIN_HW, SIDE - SHIFT_HW - WIN_HW),
    (0, SHIFT_HW),
)
ACROSS = 2 * WIN_HW - 1
RECTS = (
    (0, 0, True, 0),
    (1, 0, True, 0),
    (0, 1, False, 1),
    (2, 0, True, 0),
    (0, 2, False, 1),
    (2, 2, True, 3),
    (2, 1, True, 2),
    (1, 2, True, 3),
    (1, 1, True, 2),
)
BIAS_DIMS = ((7, 7), (4, 7), (4, 4), (4, 3))


def up_to(value, unit):
    return -(-value // unit) * unit


class Rect:
    pass


def plan_rects():
    rects, slots, start = [], [], 0
    class_rows = [0, 0, 0]
    for row_span, col_span, rows_outer, table in RECTS:
        r0, rn = SPANS[row_span]
        c0, cn = SPANS[col_span]
        rect = Rect()
        if rows_outer:
            places = [(r0 + a, c0 + b) for a in range(rn) for b in range(cn)]
        else:
            places = [(r0 + b, c0 + a) for a in range(cn) for b in range(rn)]
        rect.count = len(places) * WT
        rect.rows = up_to(rect.count, 16)
        rect.lanes = up_to(rect.count, 128)
        rect.start = start
        rect.table = table
        rect.kind = {512: 0, 256: 1, 128: 2}[rect.lanes]
        rect.kind_row = class_rows[rect.kind]
        class_rows[rect.kind] += rect.rows
        slots += places + [None] * ((rect.rows - rect.count) // WT)
        start += rect.rows
        rects.append(rect)
    return rects, slots, class_rows


RECT, SLOTS, KIND_ROWS = plan_rects()
TOKENS = len(SLOTS) * WT
KIND_LANES = (512, 256, 128)
PLACES = SIDE * SIDE


def nn(a, b):
    return lax.dot_general(a, b, (((1,), (0,)), ((), ())), preferred_element_type=F32)


def nt(a, b):
    return lax.dot_general(a, b, (((1,), (1,)), ((), ())), preferred_element_type=F32)


def wide(pattern, width):
    return jnp.concatenate([pattern] * (width // pattern.shape[-1]), axis=-1)


def by_frame(values, pattern):
    rows, width = values.shape
    scaled = values.reshape(rows // WT, WT, width) * wide(pattern, width)[None]
    return scaled.reshape(rows, width)


def column_sums(values):
    rows, width = values.shape
    return jnp.sum(values.reshape(rows // 8, 8, width), axis=0)


def row_half(shape):
    return lax.broadcasted_iota(jnp.int32, shape, 0) % WT < SHIFT_T


def turned(tile):
    return pltpu.roll(tile, SHIFT_T, 0)


def spread_message(message_ref, doubled):
    def pair(i, carry):
        both = message_ref[pl.ds(pl.multiple_of(i * 16, 16), 16), :].astype(F32)
        for k in range(2):
            tile = both[k * WT : k * WT + WT]
            low = row_half(tile.shape)
            swap = turned(tile)
            at = pl.multiple_of(i * 32 + k * 16, 16)
            doubled[pl.ds(at, WT), :] = jnp.where(low, tile, swap)
            doubled[pl.ds(at + WT, WT), :] = jnp.where(low, swap, tile)
        return carry

    lax.fori_loop(0, message_ref.shape[0] // 16, pair, 0)


def assemble_tokens(win, edge_ref, own_ref, alt_ref, above_ref, below_ref, doubled, tokens):
    @pl.when(win == 0)
    def _():
        spread_message(above_ref, doubled)

    @pl.when(win == 1)
    def _():
        spread_message(below_ref, doubled)

    width = tokens.shape[1]
    own_low = row_half((WT, width)) == (win == 0)
    edge = edge_ref[win] == 1
    for slot, place in enumerate(SLOTS):
        rows = slice(slot * WT, slot * WT + WT)
        if place is None:
            tokens[rows, :] = jnp.zeros((WT, width), F32)
            continue
        h, w = place
        at = (h * SIDE + w) * WT
        own = turned(own_ref[0, h, w].astype(F32))
        other = jnp.where(edge, alt_ref[0, h, w].astype(F32), doubled[at : at + WT, :])
        tokens[rows, :] = jnp.where(own_low, own, other)


def pack_message(win, tokens, first, count, message_ref):
    def pair(i, carry):
        both = tokens[pl.ds(pl.multiple_of(first + i * 32, 16), 32), :]
        tiles = []
        for k in range(2):
            one, two = both[k * 16 : k * 16 + WT], both[k * 16 + WT : k * 16 + 16]
            low = row_half(one.shape)
            late = jnp.where(low, turned(one), two)
            early = jnp.where(low, one, turned(two))
            tiles.append(jnp.where(win == 0, late, early))
        message_ref[pl.ds(pl.multiple_of(i * 16, 16), 16), :] = jnp.concatenate(tiles, axis=0).astype(
            message_ref.dtype
        )
        return carry

    lax.fori_loop(0, count // 32, pair, 0)


def spread_table(source, outer, inner, out_ref, lane):
    width = inner * WT
    total = outer * width
    for ok in range(outer):
        for ik in range(inner):
            pieces = []
            for oq in range(outer):
                shift = (oq * width - (WIN_HW - 1 - ik) * WT) % 128
                piece = source[oq - ok + WIN_HW - 1]
                pieces.append(pltpu.roll(piece, shift, 1) if shift else piece)
            row = (ok * inner + ik) * WT
            for tile in range(up_to(total, 128) // 128):
                value = None
                for oq in range(outer):
                    begin, end = oq * width, (oq + 1) * width
                    if end <= tile * 128 or begin >= tile * 128 + 128:
                        continue
                    if value is None:
                        value = pieces[oq]
                    else:
                        value = jnp.where(lane >= begin - tile * 128, pieces[oq], value)
                out_ref[0, row : row + WT, tile * 128 : tile * 128 + 128] = value


def split3(values):
    parts = []
    for _ in range(3):
        part = values.astype(BF16)
        parts.append(part)
        values = values - part.astype(F32)
    return parts


def hot_times(tk):
    count = ACROSS * (2 * WT - 1)
    place = lax.broadcasted_iota(jnp.int32, (count, 128), 0)
    lane = lax.broadcasted_iota(jnp.int32, (count, 128), 1)
    return ((lane // WT) * (2 * WT - 1) + lane % WT - tk + WT - 1 == place).astype(BF16)


def bias_kernel(rows_ref, cols_ref, b0_ref, b1_ref, b2_ref, b3_ref, strips):
    head = pl.program_id(0)

    @pl.when(head == 0)
    def _():
        for kind, table_ref in enumerate((rows_ref, cols_ref)):
            parts = split3(table_ref[...] * LOG2E)
            for tk in range(WT):
                hot = hot_times(tk)
                strips[kind, pl.ds(tk, table_ref.shape[0], stride=WT), :] = sum(nn(p, hot) for p in parts)

    lane = lax.broadcasted_iota(jnp.int32, (WT, 128), 1)
    base = pl.multiple_of(head * (ACROSS * WT), WT)
    by_rows = [strips[0, pl.ds(base + d * WT, WT), :] for d in range(ACROSS)]
    by_cols = [strips[1, pl.ds(base + d * WT, WT), :] for d in range(ACROSS)]
    for out_ref, source, (outer, inner) in zip(
        (b0_ref, b1_ref, b2_ref, b3_ref), (by_rows, by_cols, by_rows, by_rows), BIAS_DIMS
    ):
        spread_table(source, outer, inner, out_ref, lane)


def bias_shapes(heads):
    shapes = []
    for outer, inner in BIAS_DIMS:
        count = outer * inner * WT
        shapes.append((heads, count, up_to(count, 128)))
    return shapes


def make_bias(rel_table):
    heads = rel_table.shape[1]
    times = 2 * WT - 1
    cube = rel_table.T.reshape(heads, times, ACROSS, ACROSS)
    by_rows = cube.transpose(0, 2, 3, 1).reshape(heads * ACROSS, ACROSS * times)
    by_cols = cube.transpose(0, 3, 2, 1).reshape(heads * ACROSS, ACROSS * times)
    shapes = bias_shapes(heads)
    return pl.pallas_call(
        bias_kernel,
        grid=(heads,),
        in_specs=[whole(by_rows.shape), whole(by_cols.shape)],
        out_specs=[pl.BlockSpec((1,) + s[1:], lambda h: (h, 0, 0)) for s in shapes],
        out_shape=[jax.ShapeDtypeStruct(s, F32) for s in shapes],
        scratch_shapes=[pltpu.VMEM((2, heads * ACROSS * WT, 128), F32)],
        compiler_params=pltpu.CompilerParams(vmem_limit_bytes=48 << 20),
        cost_estimate=cost(10),
        name="position_bias",
    )(by_rows, by_cols)


def fold_table(acc, outer, inner, totals, lane):
    width = inner * WT
    for ok in range(outer):
        for ik in range(inner):
            row = (ok * inner + ik) * WT
            for oq in range(outer):
                shift = (oq * width - (WIN_HW - 1 - ik) * WT) % 128
                begin, end = oq * width, (oq + 1) * width
                tile, lo = begin // 128, begin % 128
                last = (end - 1) // 128
                value = acc(row, tile)
                if last == tile:
                    value = jnp.where((lane >= lo) & (lane < lo + width), value, 0.0)
                else:
                    after = jnp.where(lane < end - last * 128, acc(row, last), 0.0)
                    value = jnp.where(lane >= lo, value, after)
                d = oq - ok + WIN_HW - 1
                back = pltpu.roll(value, (128 - shift) % 128, 1) if shift else value
                totals[d] = totals[d] + back


def qkv_kernel(
    tile,
    scale,
    edge_ref,
    own_ref,
    alt_ref,
    above_ref,
    below_ref,
    gain_ref,
    bias_ref,
    w_ref,
    wb_ref,
    x_ref,
    n_ref,
    q_ref,
    k_ref,
    v_ref,
    doubled,
    tokens,
):
    win, step = pl.program_id(0), pl.program_id(1)

    @pl.when(step == 0)
    def _():
        assemble_tokens(win, edge_ref, own_ref, alt_ref, above_ref, below_ref, doubled, tokens)

    x = tokens[pl.ds(pl.multiple_of(step * tile, 16), tile), :]
    x_ref[0] = x.astype(BF16)
    unit, _ = norm_stats(x)
    n_ref[0] = unit.astype(BF16)
    normed = (unit * gain_ref[...] + bias_ref[...]).astype(BF16)
    width = x.shape[1]
    q_ref[0] = ((nn(normed, w_ref[:, :width]) + wb_ref[:, :width]) * scale).astype(BF16)
    k_ref[0] = nn(normed, w_ref[:, width : 2 * width]).astype(BF16)
    v_ref[0] = (nn(normed, w_ref[:, 2 * width :]) + wb_ref[:, 2 * width :]).astype(BF16)


def cost(micros):
    return pl.CostEstimate(flops=int(micros * 1.1e9), bytes_accessed=1 << 20, transcendentals=0)


def norm_stats(values):
    centre = values - jnp.mean(values, axis=-1, keepdims=True)
    spread = jnp.mean(centre * centre, axis=-1, keepdims=True)
    inverse = lax.rsqrt(spread + EPS)
    return centre * inverse, inverse


def norm_back(scaled, unit, inverse):
    first = jnp.mean(scaled, axis=-1, keepdims=True)
    second = jnp.mean(scaled * unit, axis=-1, keepdims=True)
    return (scaled - first - unit * second) * inverse


def whole(shape):
    return pl.BlockSpec(shape, lambda *_: (0,) * len(shape))


def scalars():
    return pl.BlockSpec(memory_space=pltpu.SMEM)


def volume_specs(width):
    block = (1, SIDE, SIDE, WT, width)
    return [
        pl.BlockSpec(block, lambda w, *_: (w, 0, 0, 0, 0)),
        pl.BlockSpec(block, lambda w, *_: (1 - w, 0, 0, 0, 0)),
        whole((PLACES * SHIFT_T, width)),
        whole((PLACES * SHIFT_T, width)),
    ]


def tile_spec(tile, width):
    return pl.BlockSpec((1, tile, width), lambda w, j: (w, j, 0))


def make_qkv(edges, volume, above, below, gain, bias, w_qkv, qkv_bias, scale, tile=400):
    width = volume.shape[-1]
    out = jax.ShapeDtypeStruct((2, TOKENS, width), BF16)
    return pl.pallas_call(
        functools.partial(qkv_kernel, tile, scale),
        grid=(2, TOKENS // tile),
        in_specs=[scalars()]
        + volume_specs(width)
        + [whole((1, width)), whole((1, width)), whole(w_qkv.shape), whole((1, 3 * width))],
        out_specs=[tile_spec(tile, width)] * 5,
        out_shape=[out] * 5,
        scratch_shapes=[
            pltpu.VMEM((PLACES * WT, width), F32),
            pltpu.VMEM((TOKENS, width), F32),
        ],
        compiler_params=pltpu.CompilerParams(vmem_limit_bytes=60 << 20),
        cost_estimate=cost(17),
        name="norm1_qkv",
    )(edges, volume, volume, above, below, gain[None], bias[None], w_qkv, qkv_bias[None])


def head_rows(transposed, head, dim):
    rows, lanes = transposed.shape
    parts = []
    if head:
        parts.append(jnp.zeros((head * dim, lanes), transposed.dtype))
    parts.append(transposed[head * dim : head * dim + dim])
    if (head + 1) * dim < rows:
        parts.append(jnp.zeros((rows - (head + 1) * dim, lanes), transposed.dtype))
    return jnp.concatenate(parts, axis=0)


def attend_kernel(
    dim, q_ref, k_ref, v_ref, far_ref, b0, b1, b2, b3, e0_ref, e1_ref, e2_ref, o_ref, r_ref, scores
):
    biases = (b0, b1, b2, b3)
    e_refs = (e0_ref, e1_ref, e2_ref)
    far = far_ref[0]
    per = 128 // dim
    for rect in RECT:
        count, rows, lanes, start = rect.count, rect.rows, rect.lanes, rect.start
        kind_rows = slice(rect.kind_row, rect.kind_row + rows)
        e_ref = e_refs[rect.kind]
        queries = q_ref[0, start : start + lanes, :].T
        keys = k_ref[0, start : start + rows, :]
        values = v_ref[0, start : start + rows, :].T
        ones = jnp.ones((16, rows), BF16)
        wide_far = wide(far, lanes)
        outs, scales = [], []
        for head in range(per):
            raw = nn(keys, head_rows(queries, head, dim))[:count]
            raw = raw + biases[rect.table][head, :count, :lanes]
            scores[:count, :lanes] = raw
            blocks = raw.reshape(count // 8, 8, lanes)
            top = jnp.max(blocks, axis=0) - wide_far
            top = jnp.max(top, axis=0, keepdims=True) + wide_far
            exps = jnp.exp2(scores[:count, :lanes].reshape(count // 8, 8, lanes) - top[None])
            exps = exps.reshape(count, lanes).astype(BF16)
            if rows > count:
                exps = jnp.concatenate([exps, jnp.zeros((rows - count, lanes), BF16)], axis=0)
            e_ref[0, 0, kind_rows, head * lanes : head * lanes + lanes] = exps
            lhs = jnp.concatenate([values[head * dim : head * dim + dim], ones], axis=0)
            out = nn(lhs, exps)
            inverse = jnp.broadcast_to(1.0 / out[dim : dim + 1], (dim, lanes))
            outs.append(out[:dim] * inverse)
            scales.append(inverse)
        o_ref[0, start : start + rows, :] = jnp.concatenate(outs, axis=0).T[:rows].astype(BF16)
        r_ref[0, start : start + rows, :] = jnp.concatenate(scales, axis=0).T[:rows]


def head_group_specs(heads, per, biases):
    lane_tile = pl.BlockSpec((1, TOKENS, 128), lambda g, w: (w, 0, g))
    far = pl.BlockSpec((1, WT, 128), lambda g, w: (w, 0, 0))
    bias = [pl.BlockSpec((per,) + b[1:], lambda g, w: (g, 0, 0)) for b in biases]
    exps = [
        pl.BlockSpec((1, 1, KIND_ROWS[i], per * KIND_LANES[i]), lambda g, w: (w, g, 0, 0)) for i in range(3)
    ]
    return lane_tile, far, bias, exps


def exps_shapes(groups, per):
    return [jax.ShapeDtypeStruct((2, groups, KIND_ROWS[i], per * KIND_LANES[i]), BF16) for i in range(3)]


def attend(q, k, v, far, biases, dim):
    width = q.shape[-1]
    heads = width // dim
    per = 128 // dim
    groups = heads // per
    lane_tile, far_spec, bias_specs, exps_specs = head_group_specs(heads, per, [b.shape for b in biases])
    return pl.pallas_call(
        functools.partial(attend_kernel, dim),
        grid=(groups, 2),
        in_specs=[lane_tile] * 3 + [far_spec] + bias_specs,
        out_specs=exps_specs + [lane_tile, lane_tile],
        out_shape=exps_shapes(groups, per)
        + [jax.ShapeDtypeStruct((2, TOKENS, width), BF16), jax.ShapeDtypeStruct((2, TOKENS, width), F32)],
        scratch_shapes=[pltpu.VMEM((RECT[0].count, RECT[0].lanes), F32)],
        compiler_params=pltpu.CompilerParams(vmem_limit_bytes=60 << 20),
        cost_estimate=cost(55),
        name="attention",
    )(q, k, v, far, *biases)


def attend_back_kernel(
    dim,
    scale,
    q_ref,
    k_ref,
    v_ref,
    g_ref,
    o_ref,
    n_ref,
    e0_ref,
    e1_ref,
    e2_ref,
    d_ref,
    gw_ref,
    sums_ref,
    rows_ref,
    cols_ref,
    a0,
    a1,
    a2,
    a3,
    grads,
    queries,
    outgrads,
    acc_w,
    strips,
):
    win = pl.program_id(0)
    accs = (a0, a1, a2, a3)
    e_refs = (e0_ref, e1_ref, e2_ref)
    per = 128 // dim
    lane = lax.broadcasted_iota(jnp.int32, (16, 128), 1)

    @pl.when(win == 0)
    def _():
        for acc in accs:
            acc[...] = jnp.zeros_like(acc)
        acc_w[...] = jnp.zeros_like(acc_w)
        sums_ref[...] = jnp.zeros_like(sums_ref)

    for rect in RECT:
        count, rows, lanes, start = rect.count, rect.rows, rect.lanes, rect.start
        kind_rows = slice(rect.kind_row, rect.kind_row + rows)
        e_ref = e_refs[rect.kind]
        keys = k_ref[0, start : start + rows, :]
        values = v_ref[0, start : start + rows, :]
        out_grad = g_ref[0, start : start + rows, :]
        if lanes > rows:
            out_grad = jnp.concatenate([out_grad, jnp.zeros((lanes - rows, 128), BF16)], axis=0)
        query = q_ref[0, start : start + lanes, :]
        out_grad_t = out_grad.T
        out_t = o_ref[0, start : start + lanes, :].T
        keys_t = keys.T
        product = out_grad_t.astype(F32) * out_t.astype(F32)
        dqs = []
        for head in range(per):
            here = slice(head * lanes, head * lanes + lanes)
            mine = ((lane[:1] >= head * dim) & (lane[:1] < head * dim + dim)).astype(BF16)
            queries[here, :] = query * mine
            outgrads[here, :] = out_grad * mine
            inner = jnp.sum(product[head * dim : head * dim + dim], axis=0, keepdims=True)
            prob_grad = nn(values, head_rows(out_grad_t, head, dim))
            exps = e_ref[0, 0, kind_rows, here].astype(F32)
            score_grad = exps * (prob_grad - inner)
            low = score_grad.astype(BF16)
            accs[rect.table][head, :count, :lanes] += score_grad[:count]
            grads[:rows, here] = low
            dqs.append(nn(keys_t[head * dim : head * dim + dim], low))
        dq = jnp.concatenate(dqs, axis=0) * scale
        d_ref[0, start : start + rows, :128] = dq.T[:rows].astype(BF16)
        dk = nn(grads[:rows, : per * lanes], queries[: per * lanes, :])
        d_ref[0, start : start + rows, 128:256] = (dk * LN2).astype(BF16)
        dv = nn(e_ref[0, 0, kind_rows, :], outgrads[: per * lanes, :])
        d_ref[0, start : start + rows, 256:] = dv.astype(BF16)

    all_grads = d_ref[0]
    acc_w[...] += lax.dot_general(n_ref[0], all_grads, (((0,), (0,)), ((), ())), preferred_element_type=F32)
    sums_ref[...] += column_sums(all_grads.astype(F32))

    @pl.when(win == 1)
    def _():
        gw_ref[...] = acc_w[...].astype(BF16)
        lane8 = lax.broadcasted_iota(jnp.int32, (WT, 128), 1)
        for head in range(per):
            by_rows = [jnp.zeros((WT, 128), F32) for _ in range(ACROSS)]
            by_cols = [jnp.zeros((WT, 128), F32) for _ in range(ACROSS)]
            for acc, totals, (outer, inner) in zip(accs, (by_rows, by_cols, by_rows, by_rows), BIAS_DIMS):
                fold_table(
                    lambda row, tile: acc[head, row : row + WT, tile * 128 : tile * 128 + 128],
                    outer,
                    inner,
                    totals,
                    lane8,
                )
            for d in range(ACROSS):
                strips[0, (head * ACROSS + d) * WT : (head * ACROSS + d + 1) * WT, :] = by_rows[d]
                strips[1, (head * ACROSS + d) * WT : (head * ACROSS + d + 1) * WT, :] = by_cols[d]
        for kind, out_ref in enumerate((rows_ref, cols_ref)):
            total = jnp.zeros(out_ref.shape, F32)
            for tk in range(WT):
                hot = hot_times(tk)
                for part in split3(strips[kind, pl.ds(tk, per * ACROSS, stride=WT), :]):
                    total = total + nt(part, hot)
            out_ref[...] = total


def attend_back(group, q, k, v, out_grad, out, unit, exps, dim):
    width = q.shape[-1]
    per = 128 // dim
    shapes = bias_shapes(per)
    lane_tile = pl.BlockSpec((1, TOKENS, 128), lambda w: (w, 0, group))
    exps_specs = [
        pl.BlockSpec((1, 1, KIND_ROWS[i], per * KIND_LANES[i]), lambda w: (w, group, 0, 0)) for i in range(3)
    ]
    times = 2 * WT - 1
    strip = (per * ACROSS, ACROSS * times)
    most = per * RECT[0].lanes
    return pl.pallas_call(
        functools.partial(attend_back_kernel, dim, dim**-0.5),
        grid=(2,),
        in_specs=[lane_tile] * 5 + [pl.BlockSpec((1, TOKENS, width), lambda w: (w, 0, 0))] + exps_specs,
        out_specs=[
            pl.BlockSpec((1, TOKENS, 384), lambda w: (w, 0, 0)),
            whole((width, 384)),
            whole((8, 384)),
            whole(strip),
            whole(strip),
        ],
        out_shape=[
            jax.ShapeDtypeStruct((2, TOKENS, 384), BF16),
            jax.ShapeDtypeStruct((width, 384), BF16),
            jax.ShapeDtypeStruct((8, 384), F32),
            jax.ShapeDtypeStruct(strip, F32),
            jax.ShapeDtypeStruct(strip, F32),
        ],
        scratch_shapes=[pltpu.VMEM(s, F32) for s in shapes]
        + [
            pltpu.VMEM((RECT[0].rows, most), BF16),
            pltpu.VMEM((most, 128), BF16),
            pltpu.VMEM((most, 128), BF16),
            pltpu.VMEM((width, 384), F32),
            pltpu.VMEM((2, per * ACROSS * WT, 128), F32),
        ],
        compiler_params=pltpu.CompilerParams(vmem_limit_bytes=60 << 20),
        cost_estimate=cost(20),
        name="attention_back",
    )(q, k, v, out_grad, out, unit, *exps)


ERFC = (0.254829592, -0.284496736, 1.421413741, -1.453152027, 1.061405429)
ERFC_P = 0.3275911


def gelu_both(u):
    t = 1.0 / (1.0 + (ERFC_P * 0.5**0.5) * jnp.abs(u))
    bell = jnp.exp2((u * u) * (-0.5 * LOG2E))
    series = 0.5 * ERFC[4]
    for factor in ERFC[3::-1]:
        series = series * t + 0.5 * factor
    tail = series * t * bell
    area = jnp.where(u >= 0.0, 1.0 - tail, tail)
    return u * area, area + u * (bell * (1.0 / np.sqrt(2.0 * np.pi)))


def mlp_kernel(
    tile,
    steps,
    chunk,
    edge_ref,
    x_ref,
    att_ref,
    r_ref,
    own_ref,
    alt_ref,
    above_ref,
    below_ref,
    da_ref,
    dm_ref,
    wp_ref,
    pb_ref,
    g_ref,
    b_ref,
    w1_ref,
    b1_ref,
    w2_ref,
    b2_ref,
    mixed_ref,
    message_ref,
    mg_ref,
    og_ref,
    gw_ref,
    small_ref,
    fc1b_ref,
    doubled,
    tokens,
    acc_p,
    acc_1,
    acc_2,
    result,
    n2g,
):
    win, step = pl.program_id(0), pl.program_id(1)
    width = x_ref.shape[-1]

    @pl.when((win == 0) & (step == 0))
    def _():
        acc_p[...] = jnp.zeros_like(acc_p)
        acc_1[...] = jnp.zeros_like(acc_1)
        acc_2[...] = jnp.zeros_like(acc_2)
        small_ref[...] = jnp.zeros_like(small_ref)
        fc1b_ref[...] = jnp.zeros_like(fc1b_ref)

    @pl.when(step == 0)
    def _():
        assemble_tokens(win, edge_ref, own_ref, alt_ref, above_ref, below_ref, doubled, tokens)

    here = pl.ds(pl.multiple_of(step * tile, 16), tile)
    da, dm = da_ref[0], dm_ref[0]
    attended = att_ref[0]
    branch = nn(attended, wp_ref[...]) + pb_ref[...]
    middle = x_ref[0].astype(F32) + by_frame(branch, da)
    unit, inverse = norm_stats(middle)
    normed = (unit * g_ref[...] + b_ref[...]).astype(BF16)
    upstream = tokens[here, :]
    result_grad = by_frame(upstream, dm).astype(BF16)
    small_ref[0] += column_sums(result_grad.astype(F32))
    normed_t = normed.T
    result_grad_t = result_grad.T
    for at in range(0, w1_ref.shape[1], chunk):
        part = slice(at, at + chunk)
        hidden = nn(normed, w1_ref[:, part]) + b1_ref[:, part]
        active, slope = gelu_both(hidden)
        active = active.astype(BF16)
        forward = nn(active, w2_ref[part, :])
        acc_2[:, part] += nn(result_grad_t, active)
        hidden_grad = (nt(result_grad, w2_ref[part, :]) * slope).astype(BF16)
        fc1b_ref[:, part] += column_sums(hidden_grad.astype(F32))
        acc_1[:, part] += nn(normed_t, hidden_grad)
        backward = nt(hidden_grad, w1_ref[:, part])
        if at == 0:
            result[...] = forward
            n2g[...] = backward
        else:
            result[...] += forward
            n2g[...] += backward
    mixed = middle + by_frame(result[...] + b2_ref[...], dm)
    mixed_ref[0] = mixed.astype(BF16)
    tokens[here, :] = mixed
    normed_grad = n2g[...]
    small_ref[1] += column_sums(normed_grad * unit)
    small_ref[2] += column_sums(normed_grad)
    middle_grad = upstream + norm_back(normed_grad * g_ref[...], unit, inverse)
    mg_ref[0] = middle_grad
    branch_grad = by_frame(middle_grad, da).astype(BF16)
    small_ref[3] += column_sums(branch_grad.astype(F32))
    acc_p[...] += nn(attended.T, branch_grad)
    out_grad = nt(branch_grad, wp_ref[...]).astype(BF16)
    og_ref[0] = (out_grad.astype(F32) * r_ref[0]).astype(BF16)

    @pl.when(step == steps - 1)
    def _():
        pack_message(win, tokens, 0, TOKENS, message_ref.at[0])

    @pl.when((win == 1) & (step == steps - 1))
    def _():
        blocks = acc_1.shape[1] // width
        for i in range(blocks):
            part = slice(i * width, i * width + width)
            gw_ref[part, :] = acc_1[:, part].astype(BF16)
            gw_ref[(blocks + i) * width : (blocks + i + 1) * width, :] = acc_2[:, part].T.astype(BF16)
        gw_ref[2 * blocks * width :, :] = acc_p[...].astype(BF16)


def mlp(
    edges, x, att, inverse, cot, above, below, drop_attn, drop_mlp, wp, pb, g, b, w1, b1, w2, b2, tile=400, chunk=512
):
    width, hidden = w1.shape
    steps = TOKENS // tile
    frames = pl.BlockSpec((1, WT, 128), lambda w, j: (w, 0, 0))
    return pl.pallas_call(
        functools.partial(mlp_kernel, tile, steps, chunk),
        grid=(2, steps),
        in_specs=[scalars(), tile_spec(tile, width), tile_spec(tile, width), tile_spec(tile, width)]
        + volume_specs(width)
        + [
            frames,
            frames,
            whole(wp.shape),
            whole((1, width)),
            whole((1, width)),
            whole((1, width)),
            whole(w1.shape),
            whole((1, hidden)),
            whole(w2.shape),
            whole((1, width)),
        ],
        out_specs=[
            tile_spec(tile, width),
            pl.BlockSpec((1, TOKENS // 2, width), lambda w, j: (w, 0, 0)),
            tile_spec(tile, width),
            tile_spec(tile, width),
            whole((2 * hidden + width, width)),
            whole((4, 8, width)),
            whole((8, hidden)),
        ],
        out_shape=[
            jax.ShapeDtypeStruct((2, TOKENS, width), BF16),
            jax.ShapeDtypeStruct((2, TOKENS // 2, width), BF16),
            jax.ShapeDtypeStruct((2, TOKENS, width), F32),
            jax.ShapeDtypeStruct((2, TOKENS, width), BF16),
            jax.ShapeDtypeStruct((2 * hidden + width, width), BF16),
            jax.ShapeDtypeStruct((4, 8, width), F32),
            jax.ShapeDtypeStruct((8, hidden), F32),
        ],
        scratch_shapes=[
            pltpu.VMEM((PLACES * WT, width), F32),
            pltpu.VMEM((TOKENS, width), F32),
            pltpu.VMEM((width, width), F32),
            pltpu.VMEM((width, hidden), F32),
            pltpu.VMEM((width, hidden), F32),
            pltpu.VMEM((tile, width), F32),
            pltpu.VMEM((tile, width), F32),
        ],
        compiler_params=pltpu.CompilerParams(vmem_limit_bytes=63 << 20),
        cost_estimate=cost(100),
        name="mlp",
    )(
        edges,
        x,
        att,
        inverse,
        cot,
        cot,
        above,
        below,
        drop_attn,
        drop_mlp,
        wp,
        pb[None],
        g[None],
        b[None],
        w1,
        b1[None],
        w2,
        b2[None],
    )


def qkv_back_kernel(d0, d1, d2, d3, x_ref, mg_ref, w_ref, g_ref, out_ref, message_ref, tokens):
    win = pl.program_id(0)
    grads = jnp.concatenate([d[0] for d in (d0, d1, d2, d3)], axis=-1)
    normed_grad = nt(grads, w_ref[...])
    unit, inverse = norm_stats(x_ref[0].astype(F32))
    grad = mg_ref[0] + norm_back(normed_grad * g_ref[...], unit, inverse)
    out_ref[0] = grad
    tokens[...] = grad
    pack_message(win, tokens, 0, tokens.shape[0], message_ref.at[0])


def qkv_back(part, grads, x, middle_grad, w_groups, gain):
    width = x.shape[-1]
    rows = TOKENS // 2
    tile = pl.BlockSpec((1, rows, width), lambda w: (w, part, 0))
    grad = pl.BlockSpec((1, rows, 384), lambda w: (w, part, 0))

    def kernel(*refs):
        qkv_back_kernel(*refs)

    return pl.pallas_call(
        kernel,
        grid=(2,),
        in_specs=[grad] * 4 + [tile] * 2 + [whole(w_groups.shape), whole((1, width))],
        out_specs=[
            pl.BlockSpec((1, rows, width), lambda w: (w, 0, 0)),
            pl.BlockSpec((1, rows // 2, width), lambda w: (w, 0, 0)),
        ],
        out_shape=[
            jax.ShapeDtypeStruct((2, rows, width), F32),
            jax.ShapeDtypeStruct((2, rows // 2, width), BF16),
        ],
        scratch_shapes=[pltpu.VMEM((rows, width), F32)],
        compiler_params=pltpu.CompilerParams(vmem_limit_bytes=60 << 20),
        cost_estimate=cost(11),
        name="qkv_back",
    )(*grads, x, middle_grad, w_groups, gain[None])


def place_kernel(parts, edge_ref, *refs):
    vol = pl.program_id(0)
    owns, alts = refs[:parts], refs[parts : 2 * parts]
    belows, aboves = refs[2 * parts : 3 * parts], refs[3 * parts : 4 * parts]
    out_ref, doubled = refs[4 * parts :]
    size = TOKENS // parts
    for part in range(parts):

        @pl.when(vol == 0)
        def _():
            spread_message(belows[part], doubled.at[pl.ds(part * size, size)])

        @pl.when(vol == 1)
        def _():
            spread_message(aboves[part], doubled.at[pl.ds(part * size, size)])

    width = out_ref.shape[-1]
    low = row_half((WT, width)) == (vol == 0)
    edge = edge_ref[vol] == 1
    for slot, place in enumerate(SLOTS):
        if place is None:
            continue
        part, at = slot * WT // size, slot * WT % size
        own = turned(owns[part][0, at : at + WT, :].astype(F32))
        alt = alts[part][0, at : at + WT, :].astype(F32)
        other = jnp.where(edge, alt, doubled[slot * WT : slot * WT + WT, :])
        out_ref[0, place[0], place[1]] = jnp.where(low, other, own).astype(out_ref.dtype)


def to_frames(edges, tokens, belows, aboves):
    parts = len(tokens)
    size = TOKENS // parts
    width = tokens[0].shape[-1]
    dtype = tokens[0].dtype
    lanes = 256
    own = pl.BlockSpec((1, size, lanes), lambda v, c: (v, 0, c))
    alt = pl.BlockSpec((1, size, lanes), lambda v, c: (1 - v, 0, c))
    message = pl.BlockSpec((size // 2, lanes), lambda v, c: (0, c))
    return pl.pallas_call(
        functools.partial(place_kernel, parts),
        grid=(2, width // lanes),
        in_specs=[scalars()] + [own] * parts + [alt] * parts + [message] * (2 * parts),
        out_specs=pl.BlockSpec((1, SIDE, SIDE, WT, lanes), lambda v, c: (v, 0, 0, 0, c)),
        out_shape=jax.ShapeDtypeStruct((2, SIDE, SIDE, WT, width), dtype),
        scratch_shapes=[pltpu.VMEM((TOKENS, lanes), F32)],
        compiler_params=pltpu.CompilerParams(vmem_limit_bytes=60 << 20),
        cost_estimate=cost(6),
        name="to_frames",
    )(edges, *tokens, *tokens, *belows, *aboves)


def tie(value, *after):
    return lax.optimization_barrier((value,) + after)[0]


def pick(array, index, axis=0):
    return lax.dynamic_index_in_dim(array, index, axis, keepdims=False)


def add_low(*values):
    return sum(v.astype(F32) for v in values).astype(BF16)


class Sum:
    def __init__(self, buffer):
        self.n = lax.axis_size("tm")
        self.size = lax.axis_size("dp")
        self.m = self.size // 2
        dp = lax.axis_index("dp")
        self.core, self.chip, self.plane = dp % 2, dp // 2, lax.axis_index("tm")
        rows, width = buffer.shape
        self.piece = (rows // (2 * self.m * self.n), width)
        self.whole = buffer.reshape((self.m, 2, self.n) + self.piece)

    def to_core(self, values):
        return lax.ppermute(values, "dp", [(i, i ^ 1) for i in range(self.size)])

    def to_chip(self, values, s):
        return lax.ppermute(values, "dp", [(i, i ^ (2 * s)) for i in range(self.size)])

    def to_plane(self, values, s):
        return lax.ppermute(values, "tm", [(i, i ^ s) for i in range(self.n)])

    def step0(self):
        self.got = self.to_core(pick(self.whole, 1 - self.core, 1))
        return self

    def step1(self):
        mine = pick(self.whole, self.core, 1)
        parts = [add_low(pick(mine, self.chip ^ s), pick(self.got, self.chip ^ s)) for s in range(self.m)]
        self.mine = parts[0]
        self.got = [self.to_chip(parts[s], s) for s in range(1, self.m)]
        return parts[-1]

    def step2(self):
        total = add_low(self.mine, *self.got)
        parts = [pick(total, self.plane ^ s) for s in range(self.n)]
        self.mine = parts[0]
        self.got = [self.to_plane(parts[s], s) for s in range(1, self.n)]
        return parts[-1]

    def step3(self):
        self.mine = add_low(self.mine, *self.got)
        return self.mine

    def gathered(self):
        return lax.all_gather(self.mine, ("dp", "tm"), tiled=True)

    def step3_back(self):
        self.step3()
        self.got = [self.to_plane(self.mine, s) for s in range(1, self.n)]
        return self.mine

    def step4_back(self):
        self.mine = jnp.stack([self.mine] + self.got)
        self.got = [self.to_chip(self.mine, s) for s in range(1, self.m)]
        return self.mine

    def step5_back(self):
        self.mine = jnp.stack([self.mine] + self.got)
        self.other = self.to_core(self.mine)
        return self.mine


def finish_kernel(m, n, groups, ids_ref, mine_ref, other_ref, w_ref, gain_ref, bias_ref, gw_ref, lg_ref, lb_ref, extra_ref, total):
    core, chip, plane = ids_ref[0], ids_ref[1], ids_ref[2]
    rows = mine_ref.shape[1]
    for c in range(m):
        for k in range(2):
            for z in range(n):
                at = (chip ^ c) * n + (plane ^ z)
                block = jnp.where(core == k, mine_ref[at].astype(F32), other_ref[at].astype(F32))
                first = ((c * 2 + k) * n + z) * rows
                total[first : first + rows, :] = block
    width = w_ref.shape[0]
    step = total.shape[1]
    lane_sum = jnp.zeros((width, 128), F32)
    bias_sum = jnp.zeros((width, 128), F32)
    gain = gain_ref[...]
    bias = bias_ref[...]
    for g in range(groups):
        part = total[g * width : (g + 1) * width, :]
        sums = total[groups * width + g : groups * width + g + 1, :]
        grad = gain * part + bias * sums
        for third in range(3):
            lanes = slice(third * 128, third * 128 + 128)
            at = third * width + g * 128
            gw_ref[:, at : at + 128] = grad[:, lanes]
            weight = w_ref[:, at : at + 128].astype(F32)
            lane_sum = lane_sum + weight * part[:, lanes]
            bias_sum = bias_sum + weight * sums[:, lanes]
    lg_ref[...] = jnp.sum(lane_sum, axis=1, keepdims=True)
    lb_ref[...] = jnp.sum(bias_sum, axis=1, keepdims=True)
    extra_ref[...] = total[groups * width :, :]


def finish(sums, w_qkv, gain, bias):
    width = w_qkv.shape[0]
    groups = width // 128
    rows, lanes = sums.piece
    count = sums.m * sums.n
    extras = 2 * count * rows - groups * width
    ids = jnp.stack([sums.core, sums.chip, sums.plane])
    return pl.pallas_call(
        functools.partial(finish_kernel, sums.m, sums.n, groups),
        in_specs=[scalars()] + [pl.BlockSpec(memory_space=pltpu.VMEM)] * 5,
        out_specs=[pl.BlockSpec(memory_space=pltpu.VMEM)] * 4,
        out_shape=[
            jax.ShapeDtypeStruct(w_qkv.shape, F32),
            jax.ShapeDtypeStruct((width, 1), F32),
            jax.ShapeDtypeStruct((width, 1), F32),
            jax.ShapeDtypeStruct((extras, lanes), F32),
        ],
        scratch_shapes=[pltpu.VMEM((2 * count * rows, lanes), F32)],
        compiler_params=pltpu.CompilerParams(vmem_limit_bytes=60 << 20),
        cost_estimate=cost(5),
        name="finish",
    )(
        ids,
        sums.mine.reshape(count, rows, lanes),
        sums.other.reshape(count, rows, lanes),
        w_qkv,
        gain[:, None],
        bias[:, None],
    )


def neighbours():
    count = lax.axis_size("tm")
    down = [(i, i - 1) for i in range(1, count)]
    up = [(i, i + 1) for i in range(count - 1)]
    return down, up


def fetch_halves(field):
    down, up = neighbours()
    width = field.shape[-1]
    above = lax.ppermute(field[0, :, :, :SHIFT_T].reshape(PLACES * SHIFT_T, width), "tm", down)
    below = lax.ppermute(field[1, :, :, SHIFT_T:].reshape(PLACES * SHIFT_T, width), "tm", up)
    return above, below


def send_back(message):
    down, up = neighbours()
    return lax.ppermute(message[0], "tm", up), lax.ppermute(message[1], "tm", down)


def frame_facts(segments, keep):
    count = lax.axis_size("tm")
    me = lax.axis_index("tm")
    own = 2 * SHIFT_T
    first = me * own
    t = jnp.arange(SHIFT_T)
    zero, one = jnp.zeros((SHIFT_T,), jnp.int32), jnp.ones((SHIFT_T,), jnp.int32)
    top, bottom = me == count - 1, me == 0
    frames = jnp.stack(
        [
            jnp.concatenate([first + SHIFT_T + t, jnp.where(top, first + SHIFT_T + t, first + own + t)]),
            jnp.concatenate([jnp.where(bottom, t, first - SHIFT_T + t), first + t]),
        ]
    )
    volumes = jnp.stack(
        [jnp.concatenate([zero, jnp.where(top, one, zero)]), jnp.concatenate([jnp.where(bottom, zero, one), one])]
    )
    pick_frame = (frames[:, :, None] == jnp.arange(segments.shape[1])).astype(jnp.int32)
    by_volume = jnp.sum(pick_frame[:, :, None, :] * segments[None, None], axis=-1)
    segment = jnp.where(volumes == 0, by_volume[..., 0], by_volume[..., 1])
    key = segment + 8 * (frames < SHIFT_T) + 16 * volumes
    apart = (key[:, :, None] != key[:, None, :]).astype(F32) * FAR
    far = jnp.tile(apart, (1, 1, 128 // WT))
    seg_hot = (segment[:, :, None] == jnp.arange(keep.shape[2])).astype(F32)
    kept = jnp.where(volumes[:, :, None, None] == 0, keep[0], keep[1]).astype(F32)
    drops = jnp.sum(seg_hot[:, :, None, :] * kept, axis=-1) / KEEP_RATE
    drops = jnp.broadcast_to(drops[..., None], drops.shape + (128,))
    return far, drops[:, :, 0], drops[:, :, 1]


def shards(
    volume,
    segments,
    keep,
    ln1_gain,
    ln1_bias,
    w_qkv,
    q_bias,
    v_bias,
    rel_table,
    w_proj,
    proj_bias,
    ln2_gain,
    ln2_bias,
    w_fc1,
    fc1_bias,
    w_fc2,
    fc2_bias,
    cotangent,
):
    width = volume.shape[-1]
    heads = rel_table.shape[1]
    dim = width // heads
    hidden = w_fc1.shape[1]
    groups = width // 128
    me = lax.axis_index("tm")
    top, bottom = me == lax.axis_size("tm") - 1, me == 0
    edges_in = jnp.stack([top, bottom]).astype(jnp.int32)
    edges_out = jnp.stack([bottom, top]).astype(jnp.int32)
    places = volume.transpose(0, 2, 3, 1, 4)
    cot = cotangent.transpose(0, 2, 3, 1, 4)
    above, below = fetch_halves(places)
    cot_above, cot_below = fetch_halves(cot)
    far, drop_attn, drop_mlp = frame_facts(segments, keep)
    biases = make_bias(rel_table)
    qkv_bias = jnp.concatenate([q_bias, jnp.zeros_like(q_bias), v_bias])
    w_groups = w_qkv.reshape(width, 3, groups, 128).transpose(0, 2, 1, 3).reshape(width, 3 * width)
    x, unit, q, k, v = make_qkv(
        edges_in, places, above, below, ln1_gain, ln1_bias, w_qkv, qkv_bias, dim**-0.5 * LOG2E
    )
    *exps, att, inverse = attend(q, k, v, far, biases, dim)
    mixed, mixed_message, middle_grad, out_grad, g_mlp, small2, small_fc1 = mlp(
        edges_in,
        x,
        att,
        inverse,
        cot,
        cot_above,
        cot_below,
        drop_attn,
        drop_mlp,
        w_proj,
        proj_bias,
        ln2_gain,
        ln2_bias,
        w_fc1,
        fc1_bias,
        w_fc2,
        fc2_bias,
    )
    mixed_below, mixed_above = send_back(mixed_message)
    mlp_sum = Sum(g_mlp).step0()
    grads, pieces, sums, tables = [], [], [], []
    wait = mlp_sum.whole
    for group in range(groups):
        d, gw, colsum, by_rows, by_cols = attend_back(
            group, q, k, v, tie(out_grad, wait), att, unit, exps, dim
        )
        grads.append(d)
        pieces.append(gw)
        sums.append(jnp.sum(colsum, axis=0))
        tables.append((by_rows, by_cols))
        if group < 3:
            mlp_sum.got = lax.optimization_barrier((mlp_sum.got, d))[0]
            wait = (mlp_sum.step1, mlp_sum.step2, mlp_sum.step3)[group]()
    all_mlp = mlp_sum.gathered()
    times = 2 * WT - 1
    table = jnp.concatenate([t[0] for t in tables]).reshape(heads, ACROSS, ACROSS, times)
    table = table + jnp.concatenate([t[1] for t in tables]).reshape(heads, ACROSS, ACROSS, times).swapaxes(1, 2)
    table = table.transpose(0, 3, 1, 2).reshape(-1)
    extras = jnp.concatenate(
        sums + [jnp.sum(small2, axis=1).reshape(-1), jnp.sum(small_fc1, axis=0).reshape(-1), table]
    ).astype(BF16)
    lanes = 3 * 128
    unit_rows = 8 * lax.axis_size("dp") * lax.axis_size("tm")
    rows = up_to(groups * width + -(-extras.size // lanes), unit_rows)
    extras = jnp.pad(extras, (0, (rows - groups * width) * lanes - extras.size)).reshape(-1, lanes)
    qkv_sum = Sum(jnp.concatenate(pieces + [extras])).step0()
    grad0, message0 = qkv_back(0, grads, tie(x, qkv_sum.whole), middle_grad, w_groups, ln1_gain)
    below0, above0 = send_back(message0)
    qkv_sum.got = tie(qkv_sum.got, grad0)
    wait = qkv_sum.step1()
    grad1, message1 = qkv_back(1, grads, tie(x, wait, message0), middle_grad, w_groups, ln1_gain)
    below1, above1 = send_back(message1)
    qkv_sum.got = lax.optimization_barrier((qkv_sum.got, grad1))[0]
    wait = qkv_sum.step2()
    mixed_out = to_frames(edges_out, [tie(mixed, wait)], [mixed_below], [mixed_above])
    qkv_sum.got = lax.optimization_barrier((qkv_sum.got, mixed_out))[0]
    wait = qkv_sum.step3_back()
    all_mlp = tie(all_mlp, wait)
    g_fc1 = all_mlp[: hidden].reshape(hidden // width, width, width).transpose(1, 0, 2).reshape(width, hidden)
    g_fc1, g_fc2, g_proj = g_fc1.astype(F32), all_mlp[hidden : 2 * hidden].astype(F32), all_mlp[2 * hidden :].astype(F32)
    qkv_sum.got = lax.optimization_barrier((qkv_sum.got, g_fc1, g_fc2, g_proj))[0]
    wait = qkv_sum.step4_back()
    volume_grad = to_frames(edges_out, [tie(grad0, wait), grad1], [below0, below1], [above0, above1])
    qkv_sum.got = lax.optimization_barrier((qkv_sum.got, volume_grad))[0]
    qkv_sum.step5_back()
    g_qkv, ln1_g, ln1_b, extras = finish(qkv_sum, w_qkv, ln1_gain, ln1_bias)
    extras = extras.reshape(-1)
    colsum = extras[: 3 * width].reshape(groups, 3, 128)
    at = 3 * width
    small2 = extras[at : at + 4 * width].reshape(4, width)
    at += 4 * width
    fc1_b = extras[at : at + hidden]
    at += hidden
    table = extras[at : at + rel_table.size].reshape(heads, -1).T
    return (
        mixed_out.transpose(0, 3, 1, 2, 4),
        volume_grad.transpose(0, 3, 1, 2, 4),
        ln1_g[:, 0],
        ln1_b[:, 0],
        g_qkv,
        colsum[:, 0].reshape(-1),
        colsum[:, 2].reshape(-1),
        table,
        g_proj,
        small2[3],
        small2[1],
        small2[2],
        g_fc1,
        fc1_b,
        g_fc2,
        small2[0],
    )


def solution(mesh):
    split = P("dp", "tm", None, None, None)
    return jax.shard_map(
        shards,
        mesh=mesh,
        in_specs=(split, P("dp", None), P("dp", None, None)) + (P(),) * 14 + (split,),
        out_specs=(split, split) + (P(),) * 14,
        check_vma=False,
    )
```

time: 714 us -> 492 us (0.69)
  waiting for transfers between devices: 255 us -> 10.8 us
  Pallas kernels: 284 us -> 320 us
  starting transfers between devices: 24.4 us -> 58.3 us
  matrix products: 25 us -> 0 us
  local copies, waits for them, and re-layouts: 84.5 us -> 60.6 us
    psum x2 -> x0, waiting for transfers between devices: 238 us -> none  [the longest x1 127 us: shards(): g_proj, g_fc1, g_fc2 = lax.psum((g_proj, g_fc1, g_fc2), ('dp', 'tm'))]
    ppermute x8 -> x31, starting transfers between devices: 24.3 us -> 58.3 us  [the longest x9 16.4 us: to_plane(): return lax.ppermute(values, 'tm', [(i, i ^ s) for i in range(self.n)])]
    pallas_call x1 -> x4, Pallas kernels: 77.3 us -> 106 us  [attend_back(): pl.pallas_call(functools.partial(attend_back_kernel, dim, dim ** (-0.5)),...]
    dot_general x3 -> x0, matrix products: 25 us -> none  [the longest x1 11.5 us: shards(): jnp.einsum('nbkas,ksd->dabn', by_cols, time_hot(), precision=PRECISE)]
    unnamed x52 -> x74, local copies, waits for them, and re-layouts: 25.7 us -> 11 us
    mul x2 -> x0, local copies, waits for them, and re-layouts: 14.1 us -> none  [make_bias(): cube = rel_table.reshape(2 * WT - 1, ACROSS, ACROSS, heads) * LOG2E]
    pallas_call x2 -> x6, Pallas kernels: 38.3 us -> 51.8 us  [the longest x2 18.4 us: qkv_back(): pl.pallas_call(kernel, grid=(2,), in_specs=[grad] * 4 + [tile] * 2 + [who...]
    convert_element_type x3 -> x10, other arithmetic: 6.76 us -> 15.7 us  [the longest x6 7.49 us: add_low(): return sum((v.astype(F32) for v in values)).astype(BF16)]
  transfers between devices with their start and end apart: 10 -> 32, of which waited for: 3 -> 5; matrix products, arithmetic and copies ran while one was open for 11% -> 12% of each run, Pallas kernels for 1% -> 46%
where the time goes in v2:
time: 492 us; the launch traced here: 489 us
  Pallas kernels  320 us (65%)
  local copies, waits for them, and re-layouts  60.6 us (12%)
  starting transfers between devices  58.3 us (12%)
  other arithmetic  24.1 us (5%)
  between operations  15.2 us (3%)
  waiting for transfers between devices  10.8 us (2%)
    pallas_call x4, Pallas kernels, attend_back(): pl.pallas_call(functools.partial(attend_back_kernel, dim, dim ** (-0.5)),...  106 us
    pallas_call x1, Pallas kernels, mlp(): pl.pallas_call(functools.partial(mlp_kernel, tile, steps, chunk), grid=(2...  89.6 us
    pallas_call x1, Pallas kernels, attend(): pl.pallas_call(functools.partial(attend_kernel, dim), grid=(groups, 2), i...  55.4 us
    pallas_call x2, Pallas kernels, qkv_back(): pl.pallas_call(kernel, grid=(2,), in_specs=[grad] * 4 + [tile] * 2 + [who...  18.4 us
    pallas_call x2, Pallas kernels, to_frames(): pl.pallas_call(functools.partial(place_kernel, parts), grid=(2, width //...  16.8 us
    pallas_call x1, Pallas kernels, make_qkv(): pl.pallas_call(functools.partial(qkv_kernel, tile, scale), grid=(2, TOKEN...  16.8 us
    ppermute x9, starting transfers between devices, to_plane(): return lax.ppermute(values, 'tm', [(i, i ^ s) for i in range(self.n)])  16.4 us
    ppermute x3, starting transfers between devices, send_back(): lax.ppermute(message[0], 'tm', up)  12.7 us
  transfers between devices with their start and end apart: 32, of which 5 were waited for; matrix products, arithmetic and copies ran while one was open for 12% of the time, Pallas kernels for 46%

profile of v2, /device:TPU:0, one launch (start us, length us, event | category | flops | bytes accessed | tf_op | source)
XLA Modules:
  0.0 488.5 jit_solution(18280601363502820877)
XLA Ops:
  7.2 2.5 fusion.28
  13.2 6.4 %collective-permute-start.1 = (bf16[784,512]{1,0:T(8,128)(2,1)}, bf16[784,512]{1,0:T(8,128)(2,1)}, u32[]{:S(2)}, u32[]{:S(2)}) collective-permute-start(bf16[784,512]{1,0:T(8,128)(2,1)} %reshape_squeeze.19), channel_id=1, source_target_pairs={{0,1},{1,2},{2,3},{4,5},{5,6},{6,7},{8,9},{9,10},{10,11},{12,13},{... | collective-permute-start | bytes 2408456 | tf_op jit(solution)/shard_map/ppermute | solution.py:1047
  19.6 2.5 fusion.27
  24.8 5.7 %collective-permute-start.3 = (bf16[784,512]{1,0:T(8,128)(2,1)}, bf16[784,512]{1,0:T(8,128)(2,1)}, u32[]{:S(2)}, u32[]{:S(2)}) collective-permute-start(bf16[784,512]{1,0:T(8,128)(2,1)} %reshape_squeeze.21), channel_id=1, source_target_pairs={{0,1},{1,2},{2,3},{4,5},{5,6},{6,7},{8,9},{9,10},{10,11},{12,13},{... | collective-permute-start | bytes 2408456 | tf_op jit(solution)/shard_map/ppermute | solution.py:1047
  37.9 3.0 copy.83
  43.7 11.3 %position_bias.1 = (f32[16,392,512]{2,1,0:T(8,128)}, f32[16,224,256]{2,1,0:T(8,128)S(1)}, f32[16,128,128]{2,1,0:T(8,128)S(1)}, f32[16,96,128]{2,1,0:T(8,128)S(1)}) custom-call(f32[208,195]{1,0:T(8,128)S(1)} %reshape.384.rows_ref, f32[208,195]{1,0:T(8,128)S(1)} %reshape.385.cols_ref), custom_call_target="tpu_custom_call" | custom-call | flops 11000000512 | bytes 1048576 | tf_op jit(solution)/shard_map/position_bias/pallas_call | solution.py:248
  58.7 16.8 %norm1_qkv.1 = (bf16[2,1600,512]{2,1,0:T(8,128)(2,1)}, bf16[2,1600,512]{2,1,0:T(8,128)(2,1)}, bf16[2,1600,512]{2,1,0:T(8,128)(2,1)}, bf16[2,1600,512]{2,1,0:T(8,128)(2,1)}, bf16[2,1600,512]{2,1,0:T(8,128)(2,1)}) custom-call(s32[2]{0:T(128)} %add_convert_fusion.3.edge_ref, bf16[2,14,14,8,512]{4,3,2,1,0:T(8,128)(2,1)} %bitcast.189, ...), custom_call_target="tpu_custom_call" | custom-call | flops 18699999232 | bytes 1048576 | tf_op jit(solution)/shard_map/norm1_qkv/pallas_call | solution.py:361
  75.5 55.4 %attention.1 = (bf16[2,4,400,2048]{3,2,1,0:T(8,128)(2,1)}, bf16[2,4,800,1024]{3,2,1,0:T(8,128)(2,1)}, bf16[2,4,400,512]{3,2,1,0:T(8,128)(2,1)}, bf16[2,1600,512]{2,1,0:T(8,128)(2,1)}, f32[2,1600,512]{2,1,0:T(8,128)}) custom-call(bf16[2,1600,512]{2,1,0:T(8,128)(2,1)} %get-tuple-element.95.q_ref, bf16[2,1600,512]{2,1,0:T(8,128)(2,1)} %get-tuple-element.96.k_ref, ...), custom_call_target="tpu_custom_call" | custom-call | flops 60500000768 | bytes 1048576 | tf_op jit(solution)/shard_map/attention/pallas_call | solution.py:448
  132.3 89.6 %mlp.1 = (bf16[2,1600,512]{2,1,0:T(8,128)(2,1)}, bf16[2,800,512]{2,1,0:T(8,128)(2,1)}, f32[2,1600,512]{2,1,0:T(8,128)}, bf16[2,1600,512]{2,1,0:T(8,128)(2,1)}, b...) custom-call(s32[2]{0:T(128)} %add_convert_fusion.3.edge_ref, ...), custom_call_target="tpu_custom_call" | custom-call | flops 109999996928 | bytes 1048576 | tf_op jit(solution)/shard_map/mlp/pallas_call | solution.py:741
  221.9 3.3 dynamic-slice_bitcast_fusion
  225.2 26.3 %attention_back.4 = (bf16[2,1600,384]{2,1,0:T(8,128)(2,1)}, bf16[512,384]{1,0:T(8,128)(2,1)}, f32[8,384]{1,0:T(8,128)}, f32[52,195]{1,0:T(8,128)}, f32[52,195]{1,0:T(8,128)}) custom-call(bf16[2,1600,512]{2,1,0:T(8,128)(2,1)} %get-tuple-element.95.q_ref, bf16[2,1600,512]{2,1,0:T(8,128)(2,1)} %get-tuple-element.96.k_ref, ...), custom_call_target="tpu_custom_call" | custom-call | flops 22000001024 | bytes 1048576 | tf_op jit(solution)/shard_map/attention_back/pallas_call | solution.py:579
  251.5 2.9 fusion.1
  254.5 2.9 collective-permute-start.7
  257.9 26.4 %attention_back.5 = (bf16[2,1600,384]{2,1,0:T(8,128)(2,1)}, bf16[512,384]{1,0:T(8,128)(2,1)}, f32[8,384]{1,0:T(8,128)}, f32[52,195]{1,0:T(8,128)}, f32[52,195]{1,0:T(8,128)}) custom-call(bf16[2,1600,512]{2,1,0:T(8,128)(2,1)} %get-tuple-element.95.q_ref, bf16[2,1600,512]{2,1,0:T(8,128)(2,1)} %get-tuple-element.96.k_ref, ...), custom_call_target="tpu_custom_call" | custom-call | flops 22000001024 | bytes 1048576 | tf_op jit(solution)/shard_map/attention_back/pallas_call | solution.py:579
  290.7 26.6 %attention_back.6 = (bf16[2,1600,384]{2,1,0:T(8,128)(2,1)}, bf16[512,384]{1,0:T(8,128)(2,1)}, f32[8,384]{1,0:T(8,128)}, f32[52,195]{1,0:T(8,128)}, f32[52,195]{1,0:T(8,128)}) custom-call(bf16[2,1600,512]{2,1,0:T(8,128)(2,1)} %get-tuple-element.95.q_ref, bf16[2,1600,512]{2,1,0:T(8,128)(2,1)} %get-tuple-element.96.k_ref, ...), custom_call_target="tpu_custom_call" | custom-call | flops 22000001024 | bytes 1048576 | tf_op jit(solution)/shard_map/attention_back/pallas_call | solution.py:579
  323.2 3.5 collective-permute-start.15
  332.2 26.8 %attention_back.7 = (bf16[2,1600,384]{2,1,0:T(8,128)(2,1)}, bf16[512,384]{1,0:T(8,128)(2,1)}, f32[8,384]{1,0:T(8,128)}, f32[52,195]{1,0:T(8,128)}, f32[52,195]{1,0:T(8,128)}) custom-call(bf16[2,1600,512]{2,1,0:T(8,128)(2,1)} %get-tuple-element.95.q_ref, bf16[2,1600,512]{2,1,0:T(8,128)(2,1)} %get-tuple-element.96.k_ref, ...), custom_call_target="tpu_custom_call" | custom-call | flops 22000001024 | bytes 1048576 | tf_op jit(solution)/shard_map/attention_back/pallas_call | solution.py:579
  365.8 3.0 copy.74
  372.5 9.3 %qkv_back.2 = (f32[2,800,512]{2,1,0:T(8,128)}, bf16[2,400,512]{2,1,0:T(8,128)(2,1)}) custom-call(bf16[2,1600,384]{2,1,0:T(8,128)(2,1)} %get-tuple-element.113.refs_0_, bf16[2,1600,384]{2,1,0:T(8,128)(2,1)} %get-tuple-element.117.refs_1_, bf16[2,1600,384]{2,1,0:T(8,128)(2,1)} %get-tuple-element.123.refs_2_, bf16[2,1600,384]{2,1,0:T(8,128)(2,1)} %get-tuple-element.143.refs_3_, ...), custom_call_target="tpu_custom_call" | custom-call | flops 12099999744 | bytes 1048576 | tf_op jit(solution)/shard_map/qkv_back/pallas_call | solution.py:830
  386.2 9.2 %qkv_back.3 = (f32[2,800,512]{2,1,0:T(8,128)}, bf16[2,400,512]{2,1,0:T(8,128)(2,1)}) custom-call(bf16[2,1600,384]{2,1,0:T(8,128)(2,1)} %get-tuple-element.113.refs_0_, bf16[2,1600,384]{2,1,0:T(8,128)(2,1)} %get-tuple-element.117.refs_1_, bf16[2,1600,384]{2,1,0:T(8,128)(2,1)} %get-tuple-element.123.refs_2_, bf16[2,1600,384]{2,1,0:T(8,128)(2,1)} %get-tuple-element.143.refs_3_, ...), custom_call_target="tpu_custom_call" | custom-call | flops 12099999744 | bytes 1048576 | tf_op jit(solution)/shard_map/qkv_back/pallas_call | solution.py:830
  398.6 4.6 collective-permute-done.12
  403.2 5.2 %collective-permute-start.23 = (bf16[400,512]{1,0:T(8,128)(2,1)S(1)}, bf16[400,512]{1,0:T(8,128)(2,1)}, u32[]{:S(2)}, u32[]{:S(2)}) collective-permute-start(bf16[400,512]{1,0:T(8,128)(2,1)S(1)} %get-tuple-element.191), channel_id=1, source_target_pairs={{0,1},{1,2},{2,3},{4,5},{5,6},{6,7},{8,9},{9,10},{10,11},{12,13},{... | collective-permute-start | bytes 1228808 | tf_op jit(solution)/shard_map/ppermute | solution.py:1053
  410.8 4.0 collective-permute-start.19
  415.5 7.2 %to_frames.2 = bf16[2,14,14,8,512]{4,3,2,1,0:T(8,128)(2,1)} custom-call(s32[2]{0:T(128)} %add_convert_fusion.2.edge_ref, bf16[2,1600,512]{2,1,0:T(8,128)(2,1)} %get-tuple-element.154.refs_0_.refs_1_, bf16[2,1600,512]{2,1,0:T(8,128)(2,1)} %get-tuple-element.154.refs_0_.refs_1_, bf16[800,512]{1,0:T(8,128)(2,1)} %collective-permute-done.15.refs_2_, ...), custom_call_target="tpu_custom_call" | custom-call | flops 6600000000 | bytes 1048576 | tf_op jit(solution)/shard_map/to_frames/pallas_call | solution.py:887
  423.1 3.9 collective-permute-start.24
  428.4 2.7 collective-permute-start.20
  431.1 4.9 %slice_convert_fusion = (f32[2048,512]{1,0:T(8,128)}, bf16[2048,512]{1,0:T(8,128)(2,1)S(1)}) fusion(bf16[4608,512]{1,0:T(8,128)(2,1)} %all-gather.2.cloned.1.call-done), kind=kLoop, calls=%fused_computation.2 | loop fusion | flops 1048576 | bytes 10485760 | tf_op jit(solution)/shard_map/convert_element_type | solution.py:1187
  436.0 3.4 collective-permute-done.20
  449.0 2.7 copy.88
  452.7 2.5 collective-permute-start.29
  455.2 9.6 %to_frames.3 = f32[2,14,14,8,512]{4,3,2,1,0:T(8,128)} custom-call(s32[2]{0:T(128)} %add_convert_fusion.2.edge_ref, f32[2,800,512]{2,1,0:T(8,128)} %get-tuple-element.163.refs_0_.refs_2_, f32[2,800,512]{2,1,0:T(8,128)} %get-tuple-element.150.refs_1_.refs_3_, f32[2,800,512]{2,1,0:T(8,128)} %get-tuple-element.163.refs_0_.refs_2_, ...), custom_call_target="tpu_custom_call" | custom-call | flops 6600000000 | bytes 1048576 | tf_op jit(solution)/shard_map/to_frames/pallas_call | solution.py:887
  468.5 5.2 %finish.1 = (f32[512,1536]{1,0:T(8,128)}, f32[512,1]{1,0:T(8,128)}, f32[512,1]{1,0:T(8,128)}, f32[256,384]{1,0:T(8,128)}) custom-call(s32[3]{0:T(128)} %pad_add_fusion.5.ids_ref, bf16[16,72,384]{2,1,0:T(8,128)(2,1)} %bitcast.187, bf16[16,72,384]{2,1,0:T(8,128)(2,1)} %bitcast.217, bf16[512,1536]{1,0:T(8,128)(2,1)} %w_ref.3, f32[512,1]{1,0:T(8,128)} %copy.80.gain_ref, ...), custom_call_target="tpu_custom_call" | custom-call | flops 5500000256 | bytes 1048576 | tf_op jit(solution)/shard_map/finish/pallas_call | solution.py:1012
  (213 shorter events, 84.0 us)
Async XLA Ops:
  7.2 423.9 %all-gather.2.cloned.1.call-start = ((), (), s32[]{:S(2)}) async-start(), calls=%async_computation | async-start | bytes 4866048 | tf_op jit(solution)/shard_map/all_gather | solution.py:955
  10.8 47.9 %collective-permute-start = (bf16[784,512]{1,0:T(8,128)(2,1)}, bf16[784,512]{1,0:T(8,128)(2,1)}, u32[]{:S(2)}, u32[]{:S(2)}) collective-permute-start(bf16[784,512]{1,0:T(8,128)(2,1)} %reshape_squeeze.18), channel_id=1, source_target_pairs={{1,0},{2,1},{3,2},{5,4},{6,5},{7,6},{9,8},{10,9},{11,10},{13,12},{... | collective-permute-start | bytes 2408456 | tf_op jit(solution)/shard_map/ppermute | solution.py:1046
  13.2 45.5 %collective-permute-start.1 = (bf16[784,512]{1,0:T(8,128)(2,1)}, bf16[784,512]{1,0:T(8,128)(2,1)}, u32[]{:S(2)}, u32[]{:S(2)}) collective-permute-start(bf16[784,512]{1,0:T(8,128)(2,1)} %reshape_squeeze.19), channel_id=1, source_target_pairs={{0,1},{1,2},{2,3},{4,5},{5,6},{6,7},{8,9},{9,10},{10,11},{12,13},{... | collective-permute-start | bytes 2408456 | tf_op jit(solution)/shard_map/ppermute | solution.py:1047
  22.4 108.5 %collective-permute-start.2 = (bf16[784,512]{1,0:T(8,128)(2,1)S(1)}, bf16[784,512]{1,0:T(8,128)(2,1)}, u32[]{:S(2)}, u32[]{:S(2)}) collective-permute-start(bf16[784,512]{1,0:T(8,128)(2,1)S(1)} %reshape_squeeze.20), channel_id=1, source_target_pairs={{1,0},{2,1},{3,2},{5,4},{6,5},{7,6},{9,8},{10,9},{11,10},{13,12},{... | collective-permute-start | bytes 2408456 | tf_op jit(solution)/shard_map/ppermute | solution.py:1046
  24.8 106.2 %collective-permute-start.3 = (bf16[784,512]{1,0:T(8,128)(2,1)}, bf16[784,512]{1,0:T(8,128)(2,1)}, u32[]{:S(2)}, u32[]{:S(2)}) collective-permute-start(bf16[784,512]{1,0:T(8,128)(2,1)} %reshape_squeeze.21), channel_id=1, source_target_pairs={{0,1},{1,2},{2,3},{4,5},{5,6},{6,7},{8,9},{9,10},{10,11},{12,13},{... | collective-permute-start | bytes 2408456 | tf_op jit(solution)/shard_map/ppermute | solution.py:1047
  225.2 26.3 %collective-permute-start.4 = (bf16[4,4,144,512]{3,2,1,0:T(8,128)(2,1)}, bf16[4,4,144,512]{3,2,1,0:T(8,128)(2,1)S(1)}, u32[]{:S(2)}, u32[]{:S(2)}) collective-permute-start(bf16[4,4,144,512]{3,2,1,0:T(8,128)(2,1)} %dynamic-slice_bitcast_fusion), channel_id=1, source_target_pairs={{0,4},{4,0},{8,12},{12,8},{16,20},{20,16},{24,28},{28,24},{1,5},{5... | collective-permute-start | bytes 7077896 | tf_op jit(solution)/shard_map/ppermute | solution.py:924
  254.5 29.9 %collective-permute-start.7 = (bf16[4,144,512]{2,1,0:T(8,128)(2,1)S(1)}, bf16[4,144,512]{2,1,0:T(8,128)(2,1)S(1)}, u32[]{:S(2)}, u32[]{:S(2)}) collective-permute-start(bf16[4,144,512]{2,1,0:T(8,128)(2,1)S(1)} %get-tuple-element.176), channel_id=1, source_target_pairs={{0,24},{4,28},{8,16},{12,20},{16,8},{20,12},{24,0},{28,4},{1,25},{... | collective-permute-start | bytes 1769480 | tf_op jit(solution)/shard_map/ppermute | solution.py:927
  257.3 27.1 %collective-permute-start.5 = (bf16[4,144,512]{2,1,0:T(8,128)(2,1)}, bf16[4,144,512]{2,1,0:T(8,128)(2,1)}, u32[]{:S(2)}, u32[]{:S(2)}) collective-permute-start(bf16[4,144,512]{2,1,0:T(8,128)(2,1)} %get-tuple-element.175), channel_id=1, source_target_pairs={{0,8},{4,12},{8,0},{12,4},{16,24},{20,28},{24,16},{28,20},{1,9},{5... | collective-permute-start | bytes 1769480 | tf_op jit(solution)/shard_map/ppermute | solution.py:927
  257.9 26.5 %collective-permute-start.6 = (bf16[4,144,512]{2,1,0:T(8,128)(2,1)}, bf16[4,144,512]{2,1,0:T(8,128)(2,1)}, u32[]{:S(2)}, u32[]{:S(2)}) collective-permute-start(bf16[4,144,512]{2,1,0:T(8,128)(2,1)} %get-tuple-element.174), channel_id=1, source_target_pairs={{0,16},{4,20},{8,24},{12,28},{16,0},{20,4},{24,8},{28,12},{1,17},{... | collective-permute-start | bytes 1769480 | tf_op jit(solution)/shard_map/ppermute | solution.py:927
  286.2 31.0 %collective-permute-start.10 = (bf16[144,512]{1,0:T(8,128)(2,1)S(1)}, bf16[144,512]{1,0:T(8,128)(2,1)S(1)}, u32[]{:S(2)}, u32[]{:S(2)}) collective-permute-start(bf16[144,512]{1,0:T(8,128)(2,1)S(1)} %get-tuple-element.194), channel_id=1, source_target_pairs={{0,3},{1,2},{2,1},{3,0},{4,7},{5,6},{6,5},{7,4},{8,11},{9,10},{10,... | collective-permute-start | bytes 442376 | tf_op jit(solution)/shard_map/ppermute | solution.py:930
  288.1 29.1 %collective-permute-start.8 = (bf16[144,512]{1,0:T(8,128)(2,1)S(1)}, bf16[144,512]{1,0:T(8,128)(2,1)S(1)}, u32[]{:S(2)}, u32[]{:S(2)}) collective-permute-start(bf16[144,512]{1,0:T(8,128)(2,1)S(1)} %get-tuple-element.193), channel_id=1, source_target_pairs={{0,1},{1,0},{2,3},{3,2},{4,5},{5,4},{6,7},{7,6},{8,9},{9,8},{10,11... | collective-permute-start | bytes 442376 | tf_op jit(solution)/shard_map/ppermute | solution.py:930
  289.9 27.4 %collective-permute-start.9 = (bf16[144,512]{1,0:T(8,128)(2,1)S(1)}, bf16[144,512]{1,0:T(8,128)(2,1)S(1)}, u32[]{:S(2)}, u32[]{:S(2)}) collective-permute-start(bf16[144,512]{1,0:T(8,128)(2,1)S(1)} %get-tuple-element.192), channel_id=1, source_target_pairs={{0,2},{1,3},{2,0},{3,1},{4,6},{5,7},{6,4},{7,5},{8,10},{9,11},{10,... | collective-permute-start | bytes 442376 | tf_op jit(solution)/shard_map/ppermute | solution.py:930
  323.2 91.7 %collective-permute-start.15 = (bf16[800,512]{1,0:T(8,128)(2,1)}, bf16[800,512]{1,0:T(8,128)(2,1)}, u32[]{:S(2)}, u32[]{:S(2)}) collective-permute-start(bf16[800,512]{1,0:T(8,128)(2,1)} %get-tuple-element.187), channel_id=1, source_target_pairs={{0,1},{1,2},{2,3},{4,5},{5,6},{6,7},{8,9},{9,10},{10,11},{12,13},{... | collective-permute-start | bytes 2457608 | tf_op jit(solution)/shard_map/ppermute | solution.py:1053
  326.7 88.1 %collective-permute-start.16 = (bf16[800,512]{1,0:T(8,128)(2,1)}, bf16[800,512]{1,0:T(8,128)(2,1)}, u32[]{:S(2)}, u32[]{:S(2)}) collective-permute-start(bf16[800,512]{1,0:T(8,128)(2,1)} %get-tuple-element.186), channel_id=1, source_target_pairs={{1,0},{2,1},{3,2},{5,4},{6,5},{7,6},{9,8},{10,9},{11,10},{13,12},{... | collective-permute-start | bytes 2457608 | tf_op jit(solution)/shard_map/ppermute | solution.py:1053
  372.5 10.5 %collective-permute-start.11 = (bf16[4,4,72,384]{3,2,1,0:T(8,128)(2,1)}, bf16[4,4,72,384]{3,2,1,0:T(8,128)(2,1)S(1)}, u32[]{:S(2)}, u32[]{:S(2)}) collective-permute-start(bf16[4,4,72,384]{3,2,1,0:T(8,128)(2,1)} %dynamic-slice_bitcast_fusion.1), channel_id=1, source_target_pairs={{0,4},{4,0},{8,12},{12,8},{16,20},{20,16},{24,28},{28,24},{1,5},{5... | collective-permute-start | bytes 2654216 | tf_op jit(solution)/shard_map/ppermute | solution.py:924
  383.9 25.8 %collective-permute-start.14 = (bf16[4,72,384]{2,1,0:T(8,128)(2,1)S(1)}, bf16[4,72,384]{2,1,0:T(8,128)(2,1)}, u32[]{:S(2)}, u32[]{:S(2)}) collective-permute-start(bf16[4,72,384]{2,1,0:T(8,128)(2,1)S(1)} %get-tuple-element.183), channel_id=1, source_target_pairs={{0,24},{4,28},{8,16},{12,20},{16,8},{20,12},{24,0},{28,4},{1,25},{... | collective-permute-start | bytes 663560 | tf_op jit(solution)/shard_map/ppermute | solution.py:927
  395.4 7.8 %collective-permute-start.12 = (bf16[4,72,384]{2,1,0:T(8,128)(2,1)}, bf16[4,72,384]{2,1,0:T(8,128)(2,1)S(1)}, u32[]{:S(2)}, u32[]{:S(2)}) collective-permute-start(bf16[4,72,384]{2,1,0:T(8,128)(2,1)} %get-tuple-element.185), channel_id=1, source_target_pairs={{0,8},{4,12},{8,0},{12,4},{16,24},{20,28},{24,16},{28,20},{1,9},{5... | collective-permute-start | bytes 663560 | tf_op jit(solution)/shard_map/ppermute | solution.py:927
  396.0 12.4 %collective-permute-start.13 = (bf16[4,72,384]{2,1,0:T(8,128)(2,1)S(1)}, bf16[4,72,384]{2,1,0:T(8,128)(2,1)S(1)}, u32[]{:S(2)}, u32[]{:S(2)}) collective-permute-start(bf16[4,72,384]{2,1,0:T(8,128)(2,1)S(1)} %get-tuple-element.184), channel_id=1, source_target_pairs={{0,16},{4,20},{8,24},{12,28},{16,0},{20,4},{24,8},{28,12},{1,17},{... | collective-permute-start | bytes 663560 | tf_op jit(solution)/shard_map/ppermute | solution.py:927
  403.2 49.0 %collective-permute-start.23 = (bf16[400,512]{1,0:T(8,128)(2,1)S(1)}, bf16[400,512]{1,0:T(8,128)(2,1)}, u32[]{:S(2)}, u32[]{:S(2)}) collective-permute-start(bf16[400,512]{1,0:T(8,128)(2,1)S(1)} %get-tuple-element.191), channel_id=1, source_target_pairs={{0,1},{1,2},{2,3},{4,5},{5,6},{6,7},{8,9},{9,10},{10,11},{12,13},{... | collective-permute-start | bytes 1228808 | tf_op jit(solution)/shard_map/ppermute | solution.py:1053
  408.4 44.3 %collective-permute-start.25 = (bf16[400,512]{1,0:T(8,128)(2,1)S(1)}, bf16[400,512]{1,0:T(8,128)(2,1)}, u32[]{:S(2)}, u32[]{:S(2)}) collective-permute-start(bf16[400,512]{1,0:T(8,128)(2,1)S(1)} %get-tuple-element.190), channel_id=1, source_target_pairs={{1,0},{2,1},{3,2},{5,4},{6,5},{7,6},{9,8},{10,9},{11,10},{13,12},{... | collective-permute-start | bytes 1228808 | tf_op jit(solution)/shard_map/ppermute | solution.py:1053
  410.8 17.5 %collective-permute-start.19 = (bf16[72,384]{1,0:T(8,128)(2,1)S(1)}, bf16[72,384]{1,0:T(8,128)(2,1)S(1)}, u32[]{:S(2)}, u32[]{:S(2)}) collective-permute-start(bf16[72,384]{1,0:T(8,128)(2,1)S(1)} %get-tuple-element.203), channel_id=1, source_target_pairs={{0,3},{1,2},{2,1},{3,0},{4,7},{5,6},{6,5},{7,4},{8,11},{9,10},{10,... | collective-permute-start | bytes 165896 | tf_op jit(solution)/shard_map/ppermute | solution.py:930
  414.8 8.3 %collective-permute-start.17 = (bf16[72,384]{1,0:T(8,128)(2,1)S(1)}, bf16[72,384]{1,0:T(8,128)(2,1)S(1)}, u32[]{:S(2)}, u32[]{:S(2)}) collective-permute-start(bf16[72,384]{1,0:T(8,128)(2,1)S(1)} %get-tuple-element.202), channel_id=1, source_target_pairs={{0,1},{1,0},{2,3},{3,2},{4,5},{5,4},{6,7},{7,6},{8,9},{9,8},{10,11... | collective-permute-start | bytes 165896 | tf_op jit(solution)/shard_map/ppermute | solution.py:930
  414.9 12.1 %collective-permute-start.18 = (bf16[72,384]{1,0:T(8,128)(2,1)S(1)}, bf16[72,384]{1,0:T(8,128)(2,1)S(1)}, u32[]{:S(2)}, u32[]{:S(2)}) collective-permute-start(bf16[72,384]{1,0:T(8,128)(2,1)S(1)} %get-tuple-element.201), channel_id=1, source_target_pairs={{0,2},{1,3},{2,0},{3,1},{4,6},{5,7},{6,4},{7,5},{8,10},{9,11},{10,... | collective-permute-start | bytes 165896 | tf_op jit(solution)/shard_map/ppermute | solution.py:930
  423.1 32.1 %collective-permute-start.24 = (bf16[400,512]{1,0:T(8,128)(2,1)S(1)}, bf16[400,512]{1,0:T(8,128)(2,1)}, u32[]{:S(2)}, u32[]{:S(2)}) collective-permute-start(bf16[400,512]{1,0:T(8,128)(2,1)S(1)} %copy-done.9), channel_id=1, source_target_pairs={{0,1},{1,2},{2,3},{4,5},{5,6},{6,7},{8,9},{9,10},{10,11},{12,13},{... | collective-permute-start | bytes 1228808 | tf_op jit(solution)/shard_map/ppermute | solution.py:1053
  427.0 28.2 %collective-permute-start.26 = (bf16[400,512]{1,0:T(8,128)(2,1)S(1)}, bf16[400,512]{1,0:T(8,128)(2,1)}, u32[]{:S(2)}, u32[]{:S(2)}) collective-permute-start(bf16[400,512]{1,0:T(8,128)(2,1)S(1)} %copy-done.8), channel_id=1, source_target_pairs={{1,0},{2,1},{3,2},{5,4},{6,5},{7,6},{9,8},{10,9},{11,10},{13,12},{... | collective-permute-start | bytes 1228808 | tf_op jit(solution)/shard_map/ppermute | solution.py:1053
  428.4 11.0 %collective-permute-start.20 = (bf16[72,384]{1,0:T(8,128)(2,1)S(1)}, bf16[72,384]{1,0:T(8,128)(2,1)S(1)}, u32[]{:S(2)}, u32[]{:S(2)}) collective-permute-start(bf16[72,384]{1,0:T(8,128)(2,1)S(1)} %fusion.15), channel_id=1, source_target_pairs={{0,1},{1,0},{2,3},{3,2},{4,5},{5,4},{6,7},{7,6},{8,9},{9,8},{10,11... | collective-permute-start | bytes 165896 | tf_op jit(solution)/shard_map/ppermute | solution.py:930
  439.4 5.2 %collective-permute-start.21 = (bf16[72,384]{1,0:T(8,128)(2,1)S(1)}, bf16[72,384]{1,0:T(8,128)(2,1)S(1)}, u32[]{:S(2)}, u32[]{:S(2)}) collective-permute-start(bf16[72,384]{1,0:T(8,128)(2,1)S(1)} %fusion.15), channel_id=1, source_target_pairs={{0,2},{1,3},{2,0},{3,1},{4,6},{5,7},{6,4},{7,5},{8,10},{9,11},{10,... | collective-permute-start | bytes 165896 | tf_op jit(solution)/shard_map/ppermute | solution.py:930
  444.6 7.0 %collective-permute-start.22 = (bf16[72,384]{1,0:T(8,128)(2,1)S(1)}, bf16[72,384]{1,0:T(8,128)(2,1)S(1)}, u32[]{:S(2)}, u32[]{:S(2)}) collective-permute-start(bf16[72,384]{1,0:T(8,128)(2,1)S(1)} %fusion.15), channel_id=1, source_target_pairs={{0,3},{1,2},{2,1},{3,0},{4,7},{5,6},{6,5},{7,4},{8,11},{9,10},{10,... | collective-permute-start | bytes 165896 | tf_op jit(solution)/shard_map/ppermute | solution.py:930
  451.7 13.2 %collective-permute-start.27 = (bf16[4,72,384]{2,1,0:T(8,128)(2,1)S(1)}, bf16[4,72,384]{2,1,0:T(8,128)(2,1)S(1)}, u32[]{:S(2)}, u32[]{:S(2)}) collective-permute-start(bf16[4,72,384]{2,1,0:T(8,128)(2,1)S(1)} %get-tuple-element.200), channel_id=1, source_target_pairs={{0,8},{4,12},{8,0},{12,4},{16,24},{20,28},{24,16},{28,20},{1,9},{5... | collective-permute-start | bytes 663560 | tf_op jit(solution)/shard_map/ppermute | solution.py:927
  452.2 12.7 %collective-permute-start.28 = (bf16[4,72,384]{2,1,0:T(8,128)(2,1)S(1)}, bf16[4,72,384]{2,1,0:T(8,128)(2,1)S(1)}, u32[]{:S(2)}, u32[]{:S(2)}) collective-permute-start(bf16[4,72,384]{2,1,0:T(8,128)(2,1)S(1)} %get-tuple-element.200), channel_id=1, source_target_pairs={{0,16},{4,20},{8,24},{12,28},{16,0},{20,4},{24,8},{28,12},{1,17},{... | collective-permute-start | bytes 663560 | tf_op jit(solution)/shard_map/ppermute | solution.py:927
  452.7 12.2 %collective-permute-start.29 = (bf16[4,72,384]{2,1,0:T(8,128)(2,1)S(1)}, bf16[4,72,384]{2,1,0:T(8,128)(2,1)S(1)}, u32[]{:S(2)}, u32[]{:S(2)}) collective-permute-start(bf16[4,72,384]{2,1,0:T(8,128)(2,1)S(1)} %get-tuple-element.200), channel_id=1, source_target_pairs={{0,24},{4,28},{8,16},{12,20},{16,8},{20,12},{24,0},{28,4},{1,25},{... | collective-permute-start | bytes 663560 | tf_op jit(solution)/shard_map/ppermute | solution.py:927
  465.1 2.5 collective-permute-start.30
  (31 other events, 270.0 us)
Sparse Core Ops, SparseCore 0:
  318.2 64.8 all-gather.1
